TPU v7x, 256 devices: a whole 4x4x8 slice. The times are simulated.
256 devices in a mesh: swap: 2 (over core), ep: 128 (over x, z, y).
Axes of the slice: x: 4, y: 4, z: 8, core: 2. Of those that a mesh axis runs over, the one named last changes fastest.
Arguments:
- grad_out: bfloat16 [16384, 6144], P('ep'), may hold values from -6 to 6
- parked_inputs: bfloat16 [2, 16384, 3072], P('swap', 'ep'), may hold values from -6 to 6
- route_ids: int32 [16384, 2], P('ep'), may hold values from 0 to 7, all different within a row; in each aligned block of 128 rows (0 to 127, 128 to 255, ...) at most 34 rows name the same one
- route_probs: float32 [16384, 2], P('ep'), may hold values from 0.1 to 0.9
- flight_expert: int32 [1], replicated, may hold values from 0 to 7
- w_gate: bfloat16 [6144, 8192], P(None, 'ep'), may hold values from -0.078125 to 0.078125
- w_up: bfloat16 [6144, 8192], P(None, 'ep'), may hold values from -0.078125 to 0.078125
- w_down: bfloat16 [8192, 6144], P('ep'), may hold values from -0.0625 to 0.0625
Outputs:
- grad_in: bfloat16 [16384, 6144], P('ep', 'swap')
Inputs may be any that keep to these rules, and one draw needn't show every extreme that they name: `route_ids`: each row names 2 different experts; the rows of one device name any one expert at most 34 times.
All inputs are finite; a program needn't handle non-finite values.
Results may differ from a plain program's by a relative error of at most 0.0024.
Values may be sent and summed in bfloat16 or wider, within the bound.
A program may use at most 128 MiB of HBM per device.

v0:
```python
import jax
import jax.numpy as jnp
from jax import lax
from jax.sharding import PartitionSpec as P

CAP = 34


def partner_2(value, axis, apart):
    mask = 2**apart
    pairs = [(source, source ^ mask) for source in range(lax.axis_size(axis))]
    return lax.ppermute(value, axis, pairs)


def join_by_bit(mine, other, upper, axis):
    low_first = jnp.concatenate([mine, other], axis=axis)
    high_first = jnp.concatenate([other, mine], axis=axis)
    return jnp.where(upper == 1, high_first, low_first)


def on_device(grad_out, parked_inputs, route_ids, route_probs, flight_expert, w_gate, w_up, w_down):
    tokens_here = grad_out.shape[0]
    features = grad_out.shape[1]
    feat_half = features // 2
    half_cap = CAP // 2
    core = lax.axis_index("swap")
    ep_place = lax.axis_index("ep")
    hits = route_ids == flight_expert[0]
    weight = jnp.sum(jnp.where(hits, route_probs, jnp.float32(0.0)), axis=1)
    flags = jnp.any(hits, axis=1).astype(jnp.int32)
    ranks = jnp.cumsum(flags) - flags
    slot_ids = jnp.arange(CAP, dtype=jnp.int32)
    match = (ranks[None, :] == slot_ids[:, None]) & (flags[None, :] == 1)
    token_ids = jnp.arange(tokens_here, dtype=jnp.int32)
    slot_tok = jnp.sum(jnp.where(match, token_ids[None, :], 0), axis=1)
    valid = jnp.any(match, axis=1)
    mine_tok = lax.dynamic_slice_in_dim(slot_tok, core * half_cap, half_cap)
    mine_valid = lax.dynamic_slice_in_dim(valid, core * half_cap, half_cap)
    own_half = parked_inputs[0]
    partner = partner_2(own_half, "swap", 0)
    full_inputs = join_by_bit(own_half, partner, core, 1)
    x_rows = jnp.take(full_inputs, mine_tok, axis=0)
    zero = jnp.zeros((), jnp.bfloat16)
    x_rows = jnp.where(mine_valid[:, None], x_rows, zero)
    dy_rows = jnp.where(mine_valid[:, None], jnp.take(grad_out, mine_tok, axis=0), zero)
    nbits = lax.axis_size("ep").bit_length() - 1
    row_bits = list(range(3, nbits))
    col_bits = [0, 1, 2]
    rows_pair = (dy_rows[None], x_rows[None])
    for bit in row_bits:
        upper = ep_place // (1 << bit) % 2
        arrived = partner_2((rows_pair[0], rows_pair[1]), "ep", bit)
        rows_pair = (
            join_by_bit(rows_pair[0], arrived[0], upper, 0),
            join_by_bit(rows_pair[1], arrived[1], upper, 0),
        )
    gate_cols, up_cols, down_rows = (w_gate, w_up, w_down)
    for bit in col_bits:
        upper = ep_place // (1 << bit) % 2
        arrived = partner_2((gate_cols, up_cols, down_rows), "ep", bit)
        gate_cols = join_by_bit(gate_cols, arrived[0], upper, 1)
        up_cols = join_by_bit(up_cols, arrived[1], upper, 1)
        down_rows = join_by_bit(down_rows, arrived[2], upper, 0)
    dy_all = rows_pair[0].reshape(-1, features)
    x_all = rows_pair[1].reshape(-1, features)
    contract = (((1,), (1,)), ((), ()))
    gate = jnp.dot(x_all, gate_cols, preferred_element_type=jnp.float32)
    up = jnp.dot(x_all, up_cols, preferred_element_type=jnp.float32)
    dhid = lax.dot_general(dy_all, down_rows, contract, preferred_element_type=jnp.float32)
    sig = jax.nn.sigmoid(gate)
    d_up = (dhid * gate * sig).astype(jnp.bfloat16)
    d_gate = (dhid * up * sig * (1.0 + gate * (1.0 - sig))).astype(jnp.bfloat16)
    partial_value = lax.dot_general(d_gate, gate_cols, contract, preferred_element_type=jnp.float32)
    partial_value = partial_value + lax.dot_general(
        d_up, up_cols, contract, preferred_element_type=jnp.float32
    )
    partial_value = partial_value.reshape(-1, half_cap, features)
    for bit in reversed(row_bits):
        upper = ep_place // (1 << bit) % 2
        middle = partial_value.shape[0] // 2
        lower_part = partial_value[:middle]
        upper_part = partial_value[middle:]
        keeping = jnp.where(upper == 1, upper_part, lower_part)
        sending = jnp.where(upper == 1, lower_part, upper_part)
        partial_value = keeping + partner_2(sending.astype(jnp.bfloat16), "ep", bit).astype(
            sending.dtype
        )
    mine_sum = partial_value[0]
    keep_cols = lax.dynamic_slice_in_dim(mine_sum, core * feat_half, feat_half, 1)
    send_cols = lax.dynamic_slice_in_dim(mine_sum, (1 - core) * feat_half, feat_half, 1)
    theirs = partner_2(send_cols.astype(jnp.bfloat16), "swap", 0).astype(send_cols.dtype)
    slot_rows = join_by_bit(keep_cols, theirs, core, 0)
    contrib = jnp.einsum(
        "ct,cd->td", match.astype(jnp.float32), slot_rows, precision=lax.Precision.HIGHEST
    )
    own_grad = lax.dynamic_slice_in_dim(grad_out, core * feat_half, feat_half, 1)
    total = own_grad.astype(jnp.float32) + 0.5 * weight[:, None] * contrib
    return total.astype(jnp.bfloat16)


def solution(mesh):
    in_specs = (
        P("ep", None),
        P("swap", "ep", None),
        P("ep", None),
        P("ep", None),
        P(),
        P(None, "ep"),
        P(None, "ep"),
        P("ep", None),
    )
    out_specs = P("ep", "swap")
    return jax.shard_map(
        on_device, mesh=mesh, in_specs=in_specs, out_specs=out_specs, check_vma=False
    )
```

profile of v0, /device:TPU:1, one launch (start us, length us, event | category | flops | bytes accessed | tf_op | source)
XLA Modules:
  0.0 456.6 jit_solution(2229128773032647032)
XLA Ops:
  0.0 3.2 collective-permute-start.7
  14.9 7.8 %collective-permute-done.15 = bf16[6144,64]{0,1:T(8,128)(2,1)} collective-permute-done((bf16[6144,64]{0,1:T(8,128)(2,1)}, bf16[6144,64]{0,1:T(8,128)(2,1)}, u32[]{:S(2)}, u32[]{:S(2)}) %collective-permute-start.15) | collective-permute-done | bytes 786464 | tf_op jit(solution)/shard_map/ppermute | solution.py:12
  25.7 3.0 collective-permute-start
  28.7 10.9 %collective-permute-done.4 = bf16[64,6144]{1,0:T(8,128)(2,1)} collective-permute-done((bf16[64,6144]{1,0:T(8,128)(2,1)}, bf16[64,6144]{1,0:T(8,128)(2,1)}, u32[]{:S(2)}, u32[]{:S(2)}) %collective-permute-start.4) | collective-permute-done | bytes 786464 | tf_op jit(solution)/shard_map/ppermute | solution.py:12
  43.1 7.0 %collective-permute-start.9 = (bf16[2,17,6144]{2,0,1:T(2,128)(2,1)S(1)}, bf16[2,17,6144]{2,0,1:T(2,128)(2,1)S(1)}, u32[]{:S(2)}, u32[]{:S(2)}) collective-permute-start(bf16[2,17,6144]{2,0,1:T(2,128)(2,1)S(1)} %copy.92), channel_id=1, source_target_pairs={{0,16},{1,17},{2,18},{3,19},{4,20},{5,21},{6,22},{7,23},{8,24},{9,... | collective-permute-start | bytes 1253384 | tf_op jit(solution)/shard_map/ppermute | solution.py:12
  50.8 8.7 %collective-permute-done.9 = bf16[2,17,6144]{2,0,1:T(2,128)(2,1)S(1)} collective-permute-done((bf16[2,17,6144]{2,0,1:T(2,128)(2,1)S(1)}, bf16[2,17,6144]{2,0,1:T(2,128)(2,1)S(1)}, u32[]{:S(2)}, u32[]{:S(2)}) %collective-permute-start.9) | collective-permute-done | bytes 417824 | tf_op jit(solution)/shard_map/ppermute | solution.py:12
  61.9 8.9 %collective-permute-done.1 = bf16[2,17,6144]{2,0,1:T(2,128)(2,1)S(1)} collective-permute-done((bf16[2,17,6144]{2,0,1:T(2,128)(2,1)S(1)}, bf16[2,17,6144]{2,0,1:T(2,128)(2,1)S(1)}, u32[]{:S(2)}, u32[]{:S(2)}) %collective-permute-start.1) | collective-permute-done | bytes 417824 | tf_op jit(solution)/shard_map/ppermute | solution.py:12
  77.7 2.7 collective-permute-start.11
  80.4 9.9 %collective-permute-done.2 = bf16[4,17,6144]{2,0,1:T(4,128)(2,1)S(1)} collective-permute-done((bf16[4,17,6144]{2,0,1:T(4,128)(2,1)S(1)}, bf16[4,17,6144]{2,0,1:T(4,128)(2,1)S(1)}, u32[]{:S(2)}, u32[]{:S(2)}) %collective-permute-start.2) | collective-permute-done | bytes 835616 | tf_op jit(solution)/shard_map/ppermute | solution.py:12
  93.2 18.1 %collective-permute-start.17 = (bf16[6144,256]{0,1:T(8,128)(2,1)}, bf16[6144,256]{0,1:T(8,128)(2,1)}, u32[]{:S(2)}, u32[]{:S(2)}) collective-permute-start(bf16[6144,256]{0,1:T(8,128)(2,1)} %maximum_select_fusion.8), channel_id=1, source_target_pairs={{0,4},{1,5},{2,6},{3,7},{4,0},{5,1},{6,2},{7,3},{8,12},{9,13},{10,... | collective-permute-start | bytes 9437192 | tf_op jit(solution)/shard_map/ppermute | solution.py:12
  114.1 2.7 collective-permute-start.3
  116.9 7.5 %collective-permute-done.5 = bf16[128,6144]{1,0:T(8,128)(2,1)S(1)} collective-permute-done((bf16[128,6144]{1,0:T(8,128)(2,1)S(1)}, bf16[128,6144]{1,0:T(8,128)(2,1)S(1)}, u32[]{:S(2)}, u32[]{:S(2)}) %collective-permute-start.5) | collective-permute-done | bytes 1572896 | tf_op jit(solution)/shard_map/ppermute | solution.py:12
  128.4 29.8 %collective-permute-done.13 = bf16[6144,128]{0,1:T(8,128)(2,1)S(1)} collective-permute-done((bf16[6144,128]{0,1:T(8,128)(2,1)S(1)}, bf16[6144,128]{0,1:T(8,128)(2,1)S(1)}, u32[]{:S(2)}, u32[]{:S(2)}) %collective-permute-start.13) | collective-permute-done | bytes 1572896 | tf_op jit(solution)/shard_map/ppermute | solution.py:12
  163.2 3.9 maximum_select_fusion.5
  167.2 4.2 select_n.323
  173.9 3.8 maximum_select_fusion.4
  177.7 4.4 select_n.304
  182.1 6.3 %fusion.12 = f32[272,512]{1,0:T(8,128)S(1)} fusion(bf16[272,6144]{1,0:T(8,128)(2,1)S(1)} %copy-done.1, bf16[6144,256]{0,1:T(8,128)(2,1)} %maximum_select_fusion.8, bf16[6144,256]{0,1:T(8,128)(2,1)} %collective-permute-done.17, pred[]{:T(512)S(6)} %eq.97), kind=kOutput, calls=%fused_computation.38 | convolution fusion | flops 1739587584 | bytes 10190849 | tf_op jit(solution)/shard_map/dot_general | solution.py:67
  188.4 55.3 %collective-permute-done.6 = bf16[256,6144]{1,0:T(8,128)(2,1)} collective-permute-done((bf16[256,6144]{1,0:T(8,128)(2,1)}, bf16[256,6144]{1,0:T(8,128)(2,1)}, u32[]{:S(2)}, u32[]{:S(2)}) %collective-permute-start.6) | collective-permute-done | bytes 3145760 | tf_op jit(solution)/shard_map/ppermute | solution.py:12
  243.8 6.2 %fusion = f32[272,512]{1,0:T(8,128)S(1)} fusion(bf16[272,6144]{1,0:T(8,128)(2,1)S(1)} %copy-done.2, bf16[256,6144]{1,0:T(8,128)(2,1)} %maximum_select_fusion.6, bf16[256,6144]{1,0:T(8,128)(2,1)} %collective-permute-done.6, pred[]{:T(512)S(6)} %eq.97), kind=kOutput, calls=%fused_computation.4 | convolution fusion | flops 1739587584 | bytes 10190849 | tf_op jit(solution)/shard_map/dot_general | solution.py:69
  250.0 61.2 %collective-permute-done.14 = bf16[6144,256]{0,1:T(8,128)(2,1)} collective-permute-done((bf16[6144,256]{0,1:T(8,128)(2,1)}, bf16[6144,256]{0,1:T(8,128)(2,1)}, u32[]{:S(2)}, u32[]{:S(2)}) %collective-permute-start.14) | collective-permute-done | bytes 3145760 | tf_op jit(solution)/shard_map/ppermute | solution.py:12
  311.2 7.9 %fusion.13 = f32[272,6144]{1,0:T(8,128)} fusion(bf16[6144,256]{0,1:T(8,128)(2,1)} %maximum_select_fusion.7, bf16[6144,256]{0,1:T(8,128)(2,1)} %collective-permute-done.14, pred[]{:T(512)S(6)} %eq.97, f32[272,512]{1,0:T(8,128)S(1)} %fusion, f32[272,512]{1,0:T(8,128)S(1)} %fusion.12), kind=kOutput, calls=%fused_computation.39 | convolution fusion | flops 1740423168 | bytes 14090241 | tf_op jit(solution)/shard_map/dot_general | solution.py:74
  319.1 24.2 %convolution_add_fusion = f32[272,6144]{1,0:T(8,128)} fusion(f32[272,6144]{1,0:T(8,128)} %fusion.13, bf16[6144,256]{0,1:T(8,128)(2,1)} %maximum_select_fusion.8, bf16[6144,256]{0,1:T(8,128)(2,1)} %collective-permute-done.17, pred[]{:T(512)S(6)} %eq.97, f32[272,512]{1,0:T(8,128)} %copy-done.14, bf16[272,6144]{1,0:T(8,128)(2,1)S(1)} %copy-done.1, ...), kind=kOutput, calls=%fused_computation.2 | convolution fusion | flops 3482238976 | bytes 30408704 | tf_op jit(solution)/shard_map/dot_general | solution.py:73
  343.3 4.5 select_convert_fusion
  352.1 2.7 collective-permute-start.18
  354.8 3.3 slice_select_fusion
  360.8 26.8 %collective-permute-done.18 = bf16[8,17,6144]{2,0,1:T(8,128)(2,1)} collective-permute-done((bf16[8,17,6144]{2,0,1:T(8,128)(2,1)}, bf16[8,17,6144]{2,0,1:T(8,128)(2,1)}, u32[]{:S(2)}, u32[]{:S(2)}) %collective-permute-start.18) | collective-permute-done | bytes 1671200 | tf_op jit(solution)/shard_map/ppermute | solution.py:12
  387.6 4.8 %copy_add_fusion = f32[8,17,6144]{2,0,1:T(8,128)S(1)} fusion(f32[8,17,6144]{2,1,0:T(8,128)} %select_n.334, bf16[8,17,6144]{2,0,1:T(8,128)(2,1)} %collective-permute-done.18), kind=kLoop, calls=%fused_computation.18 | loop fusion | flops 1671168 | bytes 8355840 | tf_op jit(solution)/shard_map/add | solution.py:85
  394.3 13.6 %collective-permute-done.19 = bf16[4,17,6144]{2,0,1:T(4,128)(2,1)S(1)} collective-permute-done((bf16[4,17,6144]{2,0,1:T(4,128)(2,1)S(1)}, bf16[4,17,6144]{2,0,1:T(4,128)(2,1)S(1)}, u32[]{:S(2)}, u32[]{:S(2)}) %collective-permute-start.19) | collective-permute-done | bytes 835616 | tf_op jit(solution)/shard_map/ppermute | solution.py:12
  409.1 4.1 collective-permute-start.20
  413.3 11.7 %collective-permute-done.20 = bf16[2,17,6144]{2,0,1:T(2,128)(2,1)S(1)} collective-permute-done((bf16[2,17,6144]{2,0,1:T(2,128)(2,1)S(1)}, bf16[2,17,6144]{2,0,1:T(2,128)(2,1)S(1)}, u32[]{:S(2)}, u32[]{:S(2)}) %collective-permute-start.20) | collective-permute-done | bytes 417824 | tf_op jit(solution)/shard_map/ppermute | solution.py:12
  427.5 24.2 %collective-permute-done.21 = bf16[1,17,6144]{2,0,1:T(2,128)(2,1)S(1)} collective-permute-done((bf16[1,17,6144]{2,0,1:T(2,128)(2,1)S(1)}, bf16[1,17,6144]{2,0,1:T(2,128)(2,1)S(1)}, u32[]{:S(2)}, u32[]{:S(2)}) %collective-permute-start.21) | collective-permute-done | bytes 208928 | tf_op jit(solution)/shard_map/ppermute | solution.py:12
  (111 shorter events, 61.3 us)
Async XLA Ops:
  0.0 9.7 %collective-permute-start.7 = (bf16[128,3072]{1,0:T(8,128)(2,1)}, bf16[128,3072]{1,0:T(8,128)(2,1)}, u32[]{:S(2)}, u32[]{:S(2)}) collective-permute-start(bf16[128,3072]{1,0:T(8,128)(2,1)} %bitcast.19), channel_id=1, source_target_pairs={{0,128},{128,0},{1,129},{129,1},{2,130},{130,2},{3,131},{131,3},{4... | collective-permute-start | bytes 2359304 | tf_op jit(solution)/shard_map/ppermute | solution.py:12
  3.2 19.5 %collective-permute-start.15 = (bf16[6144,64]{0,1:T(8,128)(2,1)}, bf16[6144,64]{0,1:T(8,128)(2,1)}, u32[]{:S(2)}, u32[]{:S(2)}) collective-permute-start(bf16[6144,64]{0,1:T(8,128)(2,1)} %param.15), channel_id=1, source_target_pairs={{0,1},{1,0},{2,3},{3,2},{4,5},{5,4},{6,7},{7,6},{8,9},{9,8},{10,11... | collective-permute-start | bytes 2359304 | tf_op jit(solution)/shard_map/ppermute | solution.py:12
  3.2 36.4 %collective-permute-start.4 = (bf16[64,6144]{1,0:T(8,128)(2,1)}, bf16[64,6144]{1,0:T(8,128)(2,1)}, u32[]{:S(2)}, u32[]{:S(2)}) collective-permute-start(bf16[64,6144]{1,0:T(8,128)(2,1)} %param.17), channel_id=1, source_target_pairs={{0,1},{1,0},{2,3},{3,2},{4,5},{5,4},{6,7},{7,6},{8,9},{9,8},{10,11... | collective-permute-start | bytes 2359304 | tf_op jit(solution)/shard_map/ppermute | solution.py:12
  4.7 69.0 %collective-permute-start.12 = (bf16[6144,64]{0,1:T(8,128)(2,1)}, bf16[6144,64]{0,1:T(8,128)(2,1)}, u32[]{:S(2)}, u32[]{:S(2)}) collective-permute-start(bf16[6144,64]{0,1:T(8,128)(2,1)} %param.16), channel_id=1, source_target_pairs={{0,1},{1,0},{2,3},{3,2},{4,5},{5,4},{6,7},{7,6},{8,9},{9,8},{10,11... | collective-permute-start | bytes 2359304 | tf_op jit(solution)/shard_map/ppermute | solution.py:12
  12.2 27.4 %copy-start.5 = (bf16[64,6144]{1,0:T(8,128)(2,1)S(1)}, bf16[64,6144]{1,0:T(8,128)(2,1)}, u32[]{:S(2)}) copy-start(bf16[64,6144]{1,0:T(8,128)(2,1)} %param.17) | copy-start | bytes 2359300
  12.3 30.2 %collective-permute-start.8 = (bf16[1,17,6144]{2,1,0:T(8,128)(2,1)S(1)}, bf16[1,17,6144]{2,1,0:T(8,128)(2,1)S(1)}, u32[]{:S(2)}, u32[]{:S(2)}) collective-permute-start(bf16[1,17,6144]{2,1,0:T(8,128)(2,1)S(1)} %get-tuple-element.8), channel_id=1, source_target_pairs={{0,8},{1,9},{2,10},{3,11},{4,12},{5,13},{6,14},{7,15},{8,0},{9,1},... | collective-permute-start | bytes 626696 | tf_op jit(solution)/shard_map/ppermute | solution.py:12
  24.5 66.2 %collective-permute-start.16 = (bf16[6144,128]{0,1:T(8,128)(2,1)S(1)}, bf16[6144,128]{0,1:T(8,128)(2,1)S(1)}, u32[]{:S(2)}, u32[]{:S(2)}) collective-permute-start(bf16[6144,128]{0,1:T(8,128)(2,1)S(1)} %maximum_select_fusion.14), channel_id=1, source_target_pairs={{0,2},{1,3},{2,0},{3,1},{4,6},{5,7},{6,4},{7,5},{8,10},{9,11},{10,... | collective-permute-start | bytes 4718600 | tf_op jit(solution)/shard_map/ppermute | solution.py:12
  25.7 24.4 %collective-permute-start = (bf16[1,17,6144]{2,1,0:T(8,128)(2,1)S(1)}, bf16[1,17,6144]{2,1,0:T(8,128)(2,1)S(1)}, u32[]{:S(2)}, u32[]{:S(2)}) collective-permute-start(bf16[1,17,6144]{2,1,0:T(8,128)(2,1)S(1)} %get-tuple-element.9), channel_id=1, source_target_pairs={{0,8},{1,9},{2,10},{3,11},{4,12},{5,13},{6,14},{7,15},{8,0},{9,1},... | collective-permute-start | bytes 626696 | tf_op jit(solution)/shard_map/ppermute | solution.py:12
  41.4 83.0 %collective-permute-start.5 = (bf16[128,6144]{1,0:T(8,128)(2,1)S(1)}, bf16[128,6144]{1,0:T(8,128)(2,1)S(1)}, u32[]{:S(2)}, u32[]{:S(2)}) collective-permute-start(bf16[128,6144]{1,0:T(8,128)(2,1)S(1)} %maximum_select_fusion.11), channel_id=1, source_target_pairs={{0,2},{1,3},{2,0},{3,1},{4,6},{5,7},{6,4},{7,5},{8,10},{9,11},{10,... | collective-permute-start | bytes 4718600 | tf_op jit(solution)/shard_map/ppermute | solution.py:12
  43.1 16.4 %collective-permute-start.9 = (bf16[2,17,6144]{2,0,1:T(2,128)(2,1)S(1)}, bf16[2,17,6144]{2,0,1:T(2,128)(2,1)S(1)}, u32[]{:S(2)}, u32[]{:S(2)}) collective-permute-start(bf16[2,17,6144]{2,0,1:T(2,128)(2,1)S(1)} %copy.92), channel_id=1, source_target_pairs={{0,16},{1,17},{2,18},{3,19},{4,20},{5,21},{6,22},{7,23},{8,24},{9,... | collective-permute-start | bytes 1253384 | tf_op jit(solution)/shard_map/ppermute | solution.py:12
  50.7 20.1 %collective-permute-start.1 = (bf16[2,17,6144]{2,0,1:T(2,128)(2,1)S(1)}, bf16[2,17,6144]{2,0,1:T(2,128)(2,1)S(1)}, u32[]{:S(2)}, u32[]{:S(2)}) collective-permute-start(bf16[2,17,6144]{2,0,1:T(2,128)(2,1)S(1)} %copy.83), channel_id=1, source_target_pairs={{0,16},{1,17},{2,18},{3,19},{4,20},{5,21},{6,22},{7,23},{8,24},{9,... | collective-permute-start | bytes 1253384 | tf_op jit(solution)/shard_map/ppermute | solution.py:12
  60.6 15.0 %collective-permute-start.10 = (bf16[4,17,6144]{2,0,1:T(4,128)(2,1)S(1)}, bf16[4,17,6144]{2,0,1:T(4,128)(2,1)S(1)}, u32[]{:S(2)}, u32[]{:S(2)}) collective-permute-start(bf16[4,17,6144]{2,0,1:T(4,128)(2,1)S(1)} %copy.95), channel_id=1, source_target_pairs={{0,32},{1,33},{2,34},{3,35},{4,36},{5,37},{6,38},{7,39},{8,40},{9,... | collective-permute-start | bytes 2506760 | tf_op jit(solution)/shard_map/ppermute | solution.py:12
  71.9 18.4 %collective-permute-start.2 = (bf16[4,17,6144]{2,0,1:T(4,128)(2,1)S(1)}, bf16[4,17,6144]{2,0,1:T(4,128)(2,1)S(1)}, u32[]{:S(2)}, u32[]{:S(2)}) collective-permute-start(bf16[4,17,6144]{2,0,1:T(4,128)(2,1)S(1)} %copy.86), channel_id=1, source_target_pairs={{0,32},{1,33},{2,34},{3,35},{4,36},{5,37},{6,38},{7,39},{8,40},{9,... | collective-permute-start | bytes 2506760 | tf_op jit(solution)/shard_map/ppermute | solution.py:12
  75.5 82.7 %collective-permute-start.13 = (bf16[6144,128]{0,1:T(8,128)(2,1)S(1)}, bf16[6144,128]{0,1:T(8,128)(2,1)S(1)}, u32[]{:S(2)}, u32[]{:S(2)}) collective-permute-start(bf16[6144,128]{0,1:T(8,128)(2,1)S(1)} %maximum_select_fusion.13), channel_id=1, source_target_pairs={{0,2},{1,3},{2,0},{3,1},{4,6},{5,7},{6,4},{7,5},{8,10},{9,11},{10,... | collective-permute-start | bytes 4718600 | tf_op jit(solution)/shard_map/ppermute | solution.py:12
  77.7 84.5 %collective-permute-start.11 = (bf16[8,17,6144]{2,0,1:T(8,128)(2,1)S(1)}, bf16[8,17,6144]{2,0,1:T(8,128)(2,1)S(1)}, u32[]{:S(2)}, u32[]{:S(2)}) collective-permute-start(bf16[8,17,6144]{2,0,1:T(8,128)(2,1)S(1)} %copy.98), channel_id=1, source_target_pairs={{0,64},{1,65},{2,66},{3,67},{4,68},{5,69},{6,70},{7,71},{8,72},{9,... | collective-permute-start | bytes 5013512 | tf_op jit(solution)/shard_map/ppermute | solution.py:12
  93.2 88.9 %collective-permute-start.17 = (bf16[6144,256]{0,1:T(8,128)(2,1)}, bf16[6144,256]{0,1:T(8,128)(2,1)}, u32[]{:S(2)}, u32[]{:S(2)}) collective-permute-start(bf16[6144,256]{0,1:T(8,128)(2,1)} %maximum_select_fusion.8), channel_id=1, source_target_pairs={{0,4},{1,5},{2,6},{3,7},{4,0},{5,1},{6,2},{7,3},{8,12},{9,13},{10,... | collective-permute-start | bytes 9437192 | tf_op jit(solution)/shard_map/ppermute | solution.py:12
  114.1 57.3 %collective-permute-start.3 = (bf16[8,17,6144]{2,0,1:T(8,128)(2,1)}, bf16[8,17,6144]{2,0,1:T(8,128)(2,1)}, u32[]{:S(2)}, u32[]{:S(2)}) collective-permute-start(bf16[8,17,6144]{2,0,1:T(8,128)(2,1)} %copy.89), channel_id=1, source_target_pairs={{0,64},{1,65},{2,66},{3,67},{4,68},{5,69},{6,70},{7,71},{8,72},{9,... | collective-permute-start | bytes 5013512 | tf_op jit(solution)/shard_map/ppermute | solution.py:12
  126.8 117.0 %collective-permute-start.6 = (bf16[256,6144]{1,0:T(8,128)(2,1)}, bf16[256,6144]{1,0:T(8,128)(2,1)}, u32[]{:S(2)}, u32[]{:S(2)}) collective-permute-start(bf16[256,6144]{1,0:T(8,128)(2,1)} %maximum_select_fusion.6), channel_id=1, source_target_pairs={{0,4},{1,5},{2,6},{3,7},{4,0},{5,1},{6,2},{7,3},{8,12},{9,13},{10,... | collective-permute-start | bytes 9437192 | tf_op jit(solution)/shard_map/ppermute | solution.py:12
  160.6 150.6 %collective-permute-start.14 = (bf16[6144,256]{0,1:T(8,128)(2,1)}, bf16[6144,256]{0,1:T(8,128)(2,1)}, u32[]{:S(2)}, u32[]{:S(2)}) collective-permute-start(bf16[6144,256]{0,1:T(8,128)(2,1)} %maximum_select_fusion.7), channel_id=1, source_target_pairs={{0,4},{1,5},{2,6},{3,7},{4,0},{5,1},{6,2},{7,3},{8,12},{9,13},{10,... | collective-permute-start | bytes 9437192 | tf_op jit(solution)/shard_map/ppermute | solution.py:12
  182.1 61.7 %copy-start.2 = (bf16[272,6144]{1,0:T(8,128)(2,1)S(1)}, bf16[272,6144]{1,0:T(8,128)(2,1)}, u32[]{:S(2)}) copy-start(bf16[272,6144]{1,0:T(8,128)(2,1)} %select_n.304) | copy-start | bytes 10027012
  188.4 122.8 %copy-start.13 = (f32[272,512]{1,0:T(8,128)}, f32[272,512]{1,0:T(8,128)S(1)}, u32[]{:S(2)}) copy-start(f32[272,512]{1,0:T(8,128)S(1)} %fusion.12) | copy-start | bytes 1671172
  250.0 61.2 %copy-start.14 = (f32[272,512]{1,0:T(8,128)}, f32[272,512]{1,0:T(8,128)S(1)}, u32[]{:S(2)}) copy-start(f32[272,512]{1,0:T(8,128)S(1)} %fusion) | copy-start | bytes 1671172
  352.1 35.5 %collective-permute-start.18 = (bf16[8,17,6144]{2,0,1:T(8,128)(2,1)}, bf16[8,17,6144]{2,0,1:T(8,128)(2,1)}, u32[]{:S(2)}, u32[]{:S(2)}) collective-permute-start(bf16[8,17,6144]{2,0,1:T(8,128)(2,1)} %copy.101), channel_id=1, source_target_pairs={{0,64},{1,65},{2,66},{3,67},{4,68},{5,69},{6,70},{7,71},{8,72},{9,... | collective-permute-start | bytes 5013512 | tf_op jit(solution)/shard_map/ppermute | solution.py:12
  393.0 20.3 %copy-start.7 = (s32[128,2]{0,1:T(2,128)S(1)}, s32[128,2]{0,1:T(2,128)}, u32[]{:S(2)}) copy-start(s32[128,2]{0,1:T(2,128)} %param.12) | copy-start | bytes 3076
  393.0 20.2 %copy-start.8 = (f32[128,2]{0,1:T(2,128)S(1)}, f32[128,2]{0,1:T(2,128)}, u32[]{:S(2)}) copy-start(f32[128,2]{0,1:T(2,128)} %param.13) | copy-start | bytes 3076
  393.0 14.9 %collective-permute-start.19 = (bf16[4,17,6144]{2,0,1:T(4,128)(2,1)S(1)}, bf16[4,17,6144]{2,0,1:T(4,128)(2,1)S(1)}, u32[]{:S(2)}, u32[]{:S(2)}) collective-permute-start(bf16[4,17,6144]{2,0,1:T(4,128)(2,1)S(1)} %select_convert_fusion.1), channel_id=1, source_target_pairs={{0,32},{1,33},{2,34},{3,35},{4,36},{5,37},{6,38},{7,39},{8,40},{9,... | collective-permute-start | bytes 2506760 | tf_op jit(solution)/shard_map/ppermute | solution.py:12
  409.1 15.9 %collective-permute-start.20 = (bf16[2,17,6144]{2,0,1:T(2,128)(2,1)S(1)}, bf16[2,17,6144]{2,0,1:T(2,128)(2,1)S(1)}, u32[]{:S(2)}, u32[]{:S(2)}) collective-permute-start(bf16[2,17,6144]{2,0,1:T(2,128)(2,1)S(1)} %select_convert_fusion.2), channel_id=1, source_target_pairs={{0,16},{1,17},{2,18},{3,19},{4,20},{5,21},{6,22},{7,23},{8,24},{9,... | collective-permute-start | bytes 1253384 | tf_op jit(solution)/shard_map/ppermute | solution.py:12
  425.6 28.8 %copy-start = (bf16[128,6144]{1,0:T(8,128)(2,1)S(1)}, bf16[128,6144]{1,0:T(8,128)(2,1)}, u32[]{:S(2)}) copy-start(bf16[128,6144]{1,0:T(8,128)(2,1)} %param.10) | copy-start | bytes 4718596
  425.6 28.8 %copy-start.10 = (pred[128]{0:T(512)(128)(4,1)S(1)}, pred[128]{0:T(512)(128)(4,1)}, u32[]{:S(2)}) copy-start(pred[128]{0:T(512)(128)(4,1)} %copy-done.9) | copy-start | bytes 388
  425.6 28.8 %copy-start.12 = (s32[128]{0:T(128)S(1)}, s32[128]{0:T(128)}, u32[]{:S(2)}) copy-start(s32[128]{0:T(128)} %copy-done.11) | copy-start | bytes 1540
  426.2 25.5 %collective-permute-start.21 = (bf16[1,17,6144]{2,0,1:T(2,128)(2,1)S(1)}, bf16[1,17,6144]{2,0,1:T(2,128)(2,1)S(1)}, u32[]{:S(2)}, u32[]{:S(2)}) collective-permute-start(bf16[1,17,6144]{2,0,1:T(2,128)(2,1)S(1)} %fusion.23), channel_id=1, source_target_pairs={{0,8},{1,9},{2,10},{3,11},{4,12},{5,13},{6,14},{7,15},{8,0},{9,1},... | collective-permute-start | bytes 626696 | tf_op jit(solution)/shard_map/ppermute | solution.py:12
  452.6 1.8 collective-permute-start.22
  (6 other events, 44.0 us)
where the time goes:
time: 465 us; the launch traced here: 457 us
  waiting for transfers between devices  277 us (60%)
  starting transfers between devices  60.1 us (13%)
  matrix products  46.4 us (10%)
  other arithmetic  41.8 us (9%)
  local copies, waits for them, and re-layouts  29.3 us (6%)
    ppermute x23, waiting for transfers between devices, partner_2(): return lax.ppermute(value, axis, pairs)  277 us
    ppermute x23, starting transfers between devices, partner_2(): return lax.ppermute(value, axis, pairs)  60.1 us
    dot_general x1, matrix products, on_device(): lax.dot_general(d_gate, gate_cols, contract, preferred_element_type=jnp.f...  24.2 us
    select_n x15, other arithmetic, join_by_bit(): return jnp.where(upper == 1, high_first, low_first)  24 us
    select_n x8, local copies, waits for them, and re-layouts, join_by_bit(): return jnp.where(upper == 1, high_first, low_first)  14 us
  transfers between devices with their start and end apart: 23, of which 14 were waited for; matrix products, arithmetic and copies ran while one was open for 14% of the time, Pallas kernels for 0%

commit v1 on v0

v1 whole, which is shorter than its diff:
```python
import jax
import jax.numpy as jnp
from jax import lax
from jax.experimental import pallas as pl
from jax.experimental.pallas import tpu as pltpu
from jax.sharding import PartitionSpec as P

MESH = pl.DeviceIdType.MESH
BF16 = jnp.bfloat16
F32 = jnp.float32

CAP = 34
TOK = 128
FFD = 64
NX, NY, NZ = 4, 4, 8
MAIN = 32
ROWS = 16 * CAP
TAIL0 = 16 * MAIN
PIECES = 8
NUM_SEMS = 112
NT_DIMS = (((1,), (1,)), ((), ()))
NN_DIMS = (((1,), (0,)), ((), ()))
TN_DIMS = (((0,), (0,)), ((), ()))


def dot(a, b, dims=NN_DIMS):
    return lax.dot_general(a, b, dims, preferred_element_type=F32)


def iota(shape, dim):
    return lax.broadcasted_iota(jnp.int32, shape, dim)


def kernel(half, fe, ids, probs, grad, parked, wg, wu, wd, out,
           gbuf, pbuf, rx, rdy, tx, tdy, w0, wp, wf, acc, ps, pr, dbuf,
           sa, sb, rta, rba, rla, rra, rtb, rbb, rlb, rrb,
           sa2, sb2, rta2, rba2, rla2, rra2, rtb2, rbb2, rlb2, rrb2,
           t2, rtt, rlt, rrt, send_sem, recv_sem, local_sem):
    piece = half // PIECES
    hc = half // 2
    core = lax.axis_index("swap")
    ep = lax.axis_index("ep")
    y = ep % NY
    z = (ep // NY) % NZ
    x = ep // (NY * NZ)

    def chip(dx, dy, dz):
        place = (((x + dx + NX) % NX) * NZ + (z + dz + NZ) % NZ) * NY + (y + dy + NY) % NY
        return (core, place)

    xp, xm = chip(1, 0, 0), chip(-1, 0, 0)
    yp, ym = chip(0, 1, 0), chip(0, -1, 0)
    zp, zm = chip(0, 0, 1), chip(0, 0, -1)
    other = (1 - core, ep)

    copies = []

    def send(src, dst, device):
        k = len(copies)
        copy = pltpu.make_async_remote_copy(
            src_ref=src, dst_ref=dst, send_sem=send_sem.at[k], recv_sem=recv_sem.at[k],
            device_id=device, device_id_type=MESH)
        copies.append(copy)
        copy.start()
        return copy

    cols = pl.ds(pl.multiple_of(core * half, half), half)
    local = [
        pltpu.make_async_copy(parked.at[0], pbuf, local_sem.at[0]),
        pltpu.make_async_copy(grad.at[:, cols], gbuf, local_sem.at[1]),
        pltpu.make_async_copy(wg.at[:, cols], w0.at[0], local_sem.at[2]),
        pltpu.make_async_copy(wu.at[:, cols], w0.at[1], local_sem.at[3]),
        pltpu.make_async_copy(wd.at[:, cols], w0.at[2], local_sem.at[4]),
    ]
    barrier = pltpu.get_barrier_semaphore()
    for peer in (xp, xm, yp, ym, zp, zm, other):
        pl.semaphore_signal(barrier, inc=1, device_id=peer, device_id_type=MESH)
    for copy in local:
        copy.start()

    hits = ids[...] == fe[0]
    weight = jnp.sum(jnp.where(hits, probs[...], 0.0), axis=0, keepdims=True)
    flags = jnp.max(hits.astype(F32), axis=0, keepdims=True)
    before = (iota((TOK, TOK), 0) < iota((TOK, TOK), 1)).astype(F32).astype(BF16)
    ranks = dot(jnp.broadcast_to(flags, (16, TOK)).astype(BF16), before)[0:1]

    def match_of(slot, extra=None):
        rank_is = jnp.broadcast_to(ranks, slot.shape) == slot.astype(F32)
        m = jnp.where(rank_is, jnp.broadcast_to(flags, slot.shape), 0.0)
        if extra is not None:
            m = jnp.where(extra, m, 0.0)
        return m

    match_main = match_of(iota((MAIN, TOK), 0))
    tail_row = iota((16, TOK), 0)
    tail_slot = MAIN + tail_row % 2
    match_tail = match_of(tail_slot)
    pick = [match_of(tail_slot, tail_row // 2 == p).astype(BF16) for p in range(PIECES)]
    main16 = match_main.astype(BF16)

    def choose(src, rows, tails):
        rows[0:MAIN, :] = dot(main16, src[...]).astype(BF16)
        t = dot(pick[0], src[:, 0:piece])
        for p in range(1, PIECES):
            t = t + dot(pick[p], src[:, p * piece:(p + 1) * piece])
        tails[0:16, :] = t.astype(BF16)

    local[0].wait()
    choose(pbuf, rx, tx)
    local[1].wait()
    choose(gbuf, rdy, tdy)
    for copy in local[2:]:
        copy.wait()
    pl.semaphore_wait(barrier, 7)

    def rows_of(s, n=1):
        return pl.ds(MAIN * s, MAIN * n)

    def tails_of(s, n=1):
        return pl.ds(16 * s, 16 * n)

    px = [send(rx.at[rows_of(0)], rx.at[rows_of(3)], xp),
          send(rx.at[rows_of(0)], rx.at[rows_of(1)], xm),
          send(tx.at[tails_of(0)], tx.at[tails_of(3)], xp),
          send(tx.at[tails_of(0)], tx.at[tails_of(1)], xm)]
    pd = [send(rdy.at[rows_of(0)], rdy.at[rows_of(12)], yp),
          send(rdy.at[rows_of(0)], rdy.at[rows_of(4)], ym),
          send(tdy.at[tails_of(0)], tdy.at[tails_of(12)], yp),
          send(tdy.at[tails_of(0)], tdy.at[tails_of(4)], ym)]

    gu, dn = pl.ds(0, 2), pl.ds(2, 1)

    def ring(source, g, part, side):
        return send(source, wp.at[g, part, side], zp if side == 0 else zm)

    arrived = {}
    for part, name in ((gu, "gu"), (dn, "dn")):
        for side in (0, 1):
            arrived[0, name, side] = ring(w0.at[part], 0, part, side)

    def forward_rows(first, rows, tails, s3, s1, s2, plus, minus):
        for copy in first:
            copy.wait_recv()
        return [send(rows.at[pl.ds(MAIN * s3, 16)], rows.at[pl.ds(MAIN * s2, 16)], plus),
                send(rows.at[pl.ds(MAIN * s1 + 16, 16)], rows.at[pl.ds(MAIN * s2 + 16, 16)], minus),
                send(tails.at[tails_of(s1)], tails.at[tails_of(s2)], minus)]

    fx = forward_rows(px, rx, tx, 3, 1, 2, xp, xm)
    fd = forward_rows(pd, rdy, tdy, 12, 4, 8, yp, ym)
    for copy in fx:
        copy.wait_recv()
    px = [send(rx.at[rows_of(0, 4)], rx.at[rows_of(12, 4)], yp),
          send(rx.at[rows_of(0, 4)], rx.at[rows_of(4, 4)], ym),
          send(tx.at[tails_of(0, 4)], tx.at[tails_of(12, 4)], yp),
          send(tx.at[tails_of(0, 4)], tx.at[tails_of(4, 4)], ym)]
    for copy in fd:
        copy.wait_recv()
    pd_plus, pd_minus = [], []
    for j in range(4):
        pd_plus.append((send(rdy.at[rows_of(4 * j)], rdy.at[rows_of(4 * j + 3)], xp),
                        send(tdy.at[tails_of(4 * j)], tdy.at[tails_of(4 * j + 3)], xp)))
        pd_minus.append((send(rdy.at[rows_of(4 * j)], rdy.at[rows_of(4 * j + 1)], xm),
                         send(tdy.at[tails_of(4 * j)], tdy.at[tails_of(4 * j + 1)], xm)))

    def forward_weights(g, name, part):
        for side in (0, 1):
            arrived[g - 1, name, side].wait_recv()
            arrived[g, name, side] = ring(wp.at[g - 1, part, side], g, part, side)

    forward_weights(1, "gu", gu)

    for copy in px:
        copy.wait_recv()
    last = [send(rx.at[rows_of(12, 2)], rx.at[rows_of(8, 2)], yp),
            send(rx.at[rows_of(6, 2)], rx.at[rows_of(10, 2)], ym),
            send(tx.at[tails_of(12, 2)], tx.at[tails_of(8, 2)], yp),
            send(tx.at[tails_of(6, 2)], tx.at[tails_of(10, 2)], ym)]
    for pair in pd_plus + pd_minus:
        for copy in pair:
            copy.wait_recv()
    for j in range(4):
        s, to = (4 * j + 3, xp) if j < 2 else (4 * j + 1, xm)
        last.append(send(rdy.at[rows_of(s)], rdy.at[rows_of(4 * j + 2)], to))
        last.append(send(tdy.at[tails_of(s)], tdy.at[tails_of(4 * j + 2)], to))
    forward_weights(1, "dn", dn)
    for copy in last:
        copy.wait_recv()

    row, col = iota((MAIN, 256), 0), iota((MAIN, 256), 1)
    block = row // 2
    base = 16 * (4 * (block % 4) + block // 4) + row % 2
    for p in range(PIECES):
        e = jnp.where(col == base + 2 * p, 1.0, 0.0).astype(BF16)
        for tails, rows in ((tx, rx), (tdy, rdy)):
            rows[TAIL0:ROWS, p * piece:(p + 1) * piece] = dot(e, tails[...]).astype(BF16)

    def weights_of(g):
        if g == 0 or g == 4:
            w = w0 if g == 0 else wf
            return w[0:2].reshape(2 * FFD, half), w[2]
        return wp[g - 1, 0:2].reshape(4 * FFD, half), wp[g - 1, 2].reshape(2 * FFD, half)

    def width_of(g):
        return FFD if g in (0, 4) else 2 * FFD

    def partial_gate(g):
        wgu, _ = weights_of(g)

        @pl.loop(0, 2)
        def _(m):
            rows = pl.ds(pl.multiple_of(m * (ROWS // 2), 16), ROWS // 2)
            ps[g, rows, 0:2 * width_of(g)] = dot(rx[rows, :], wgu, NT_DIMS)

    def partial_dhid(g):
        _, wdn = weights_of(g)
        width = width_of(g)

        @pl.loop(0, 2)
        def _(m):
            rows = pl.ds(pl.multiple_of(m * (ROWS // 2), 16), ROWS // 2)
            dh = dot(rdy[rows, :], wdn, NT_DIMS)
            if width == FFD:
                dh = jnp.concatenate([dh, jnp.zeros_like(dh)], axis=1)
            ps[g, rows, 2 * width:2 * width + 128] = dh

    def exchange(g):
        used = pl.ds(0, 2 * width_of(g) + 128)
        return send(ps.at[g, :, used], pr.at[g, :, used], other)

    def finish(g, copy):
        copy.wait_recv()
        width = width_of(g)

        @pl.loop(0, ROWS // 32)
        def _(m):
            rows = pl.ds(pl.multiple_of(m * 32, 32), 32)
            total = ps[g, rows, 0:2 * width + 128] + pr[g, rows, 0:2 * width + 128]
            gate, up = total[:, 0:width], total[:, width:2 * width]
            dhid = total[:, 2 * width:3 * width]
            s = 1.0 / (1.0 + jnp.exp(-gate))
            d_up = dhid * gate * s
            d_gate = dhid * up * s * (1.0 + gate * (1.0 - s))
            dbuf[rows, 0:2 * width] = jnp.concatenate([d_gate, d_up], axis=1).astype(BF16)

    tile = 512

    def back_tiles(g, lo, hi):
        width = width_of(g)

        @pl.loop(lo // tile, hi // tile)
        def _(n):
            at = pl.ds(pl.multiple_of(n * tile, tile), tile)
            if g == 0 or g == 4:
                w = (w0 if g == 0 else wf)[0:2, :, at].reshape(2 * FFD, tile)
            else:
                w = wp[g - 1, 0:2, :, :, at].reshape(4 * FFD, tile)
            value = dot(dbuf[:, 0:2 * width], w)
            if g == 0:
                acc[:, at] = value
            else:
                acc[:, at] += value

    def group(g):
        partial_gate(g)
        partial_dhid(g)
        copy = exchange(g)
        finish(g, copy)
        back_tiles(g, 0, half)

    group(0)
    group(1)
    forward_weights(2, "gu", gu)
    forward_weights(2, "dn", dn)
    group(2)

    def forward_far(name, part):
        result = []
        for side in (0, 1):
            arrived[2, name, side].wait_recv()
            hid = pl.ds(32 * side, 32)
            result.append(send(wp.at[2, part, side, hid], wf.at[part, hid], zp if side == 0 else zm))
        return result

    far_gu = forward_far("gu", gu)
    partial_gate(3)
    far_dn = forward_far("dn", dn)
    partial_dhid(3)
    copy = exchange(3)
    finish(3, copy)
    back_tiles(3, 0, half)
    for copy in far_gu:
        copy.wait_recv()
    partial_gate(4)
    for copy in far_dn:
        copy.wait_recv()
    partial_dhid(4)
    copy = exchange(4)
    finish(4, copy)

    def add(a, b):
        return (a.astype(F32) + b.astype(F32)).astype(BF16)

    def start_ring(unit, h, top, bottom, left, right, plus, minus):
        size = unit.shape[1]
        up, down = pl.ds(0, h), pl.ds(h, size - h)
        return [send(unit.at[2, up], top, plus), send(unit.at[2, down], bottom, minus),
                send(unit.at[1, down], left.at[down], plus), send(unit.at[3, up], right.at[up], minus)]

    def turn_ring(begun, unit, h, top, bottom, left, right, plus, minus):
        size = unit.shape[1]
        up, down = pl.ds(0, h), pl.ds(h, size - h)
        begun[0].wait_recv()
        unit[1, up] = add(unit[1, up], top[...])
        ends = [begun[2], begun[3], send(unit.at[1, up], left.at[up], plus)]
        begun[1].wait_recv()
        unit[3, down] = add(unit[3, down], bottom[...])
        ends.append(send(unit.at[3, down], right.at[down], minus))
        return ends

    back_tiles(4, hc, half)
    for j in (2, 1, 3, 0):
        sb[j] = acc[128 * j:128 * j + 128, hc:half].astype(BF16)
    ring_b = (sb, 64, rtb, rbb, rlb, rrb, yp, ym)
    begun_b = start_ring(*ring_b)
    back_tiles(4, 0, hc)
    for i in (2, 1, 3, 0):
        for j in range(4):
            s = 4 * j + i
            sa[i, 32 * j:32 * j + 32] = acc[MAIN * s:MAIN * s + MAIN, 0:hc].astype(BF16)
        t = acc[TAIL0 + 8 * i:TAIL0 + 8 * i + 8, :]
        sa[i, 128:144] = jnp.concatenate([t[:, 0:hc], t[:, hc:half]], axis=0).astype(BF16)
    ring_a = (sa, 64, rta, rba, rla, rra, xp, xm)
    begun_a = start_ring(*ring_a)
    ends_b = turn_ring(begun_b, *ring_b)
    ends_a = turn_ring(begun_a, *ring_a)

    for copy in ends_b:
        copy.wait_recv()
    for i in range(4):
        rows = slice(32 * i, 32 * i + 32)
        sb2[i] = (sb[0, rows].astype(F32) + rlb[rows].astype(F32) + rrb[rows].astype(F32)).astype(BF16)
    ring_b2 = (sb2, 16, rtb2, rbb2, rlb2, rrb2, xp, xm)
    begun_b2 = start_ring(*ring_b2)
    for copy in ends_a:
        copy.wait_recv()
    for j in range(4):
        rows = slice(32 * j, 32 * j + 32)
        sa2[j] = (sa[0, rows].astype(F32) + rla[rows].astype(F32) + rra[rows].astype(F32)).astype(BF16)
    ring_a2 = (sa2, 16, rta2, rba2, rla2, rra2, yp, ym)
    begun_a2 = start_ring(*ring_a2)
    tail = (sa[0, 128:144].astype(F32) + rla[128:144].astype(F32) + rra[128:144].astype(F32)).astype(BF16)
    row, col = iota((64, 16), 0), iota((64, 16), 1)
    p_of = (row % 16) // 2
    wanted = 8 * (p_of // 4) + 2 * (row // 16) + row % 2
    packed = jnp.zeros((64, piece), F32)
    for q in range(4):
        f = jnp.where((col == wanted) & (p_of % 4 == q), 1.0, 0.0).astype(BF16)
        packed = packed + dot(f, tail[:, q * piece:(q + 1) * piece])
    t2[...] = packed.astype(BF16).reshape(4, 16, piece)
    tail_far = send(t2.at[2], rtt, yp)
    tail_right = send(t2.at[3], rrt, ym)
    ends_b2 = turn_ring(begun_b2, *ring_b2)
    ends_a2 = turn_ring(begun_a2, *ring_a2)
    tail_far.wait_recv()
    t2[1] = add(t2[1], rtt[...])
    tail_left = send(t2.at[1], rlt, yp)

    slot_weight = 0.5 * jnp.sum(match_main * weight, axis=1, keepdims=True)
    tail_weight = 0.5 * jnp.sum(match_tail * weight, axis=1, keepdims=True)
    for copy in ends_b2 + ends_a2 + [tail_right, tail_left]:
        copy.wait_recv()
    tail = (t2[0].astype(F32) + rlt[...].astype(F32) + rrt[...].astype(F32)) * tail_weight
    for p in range(PIECES):
        at = slice(p * piece, (p + 1) * piece)
        own, left, right = (sa2, rla2, rra2) if p < 4 else (sb2, rlb2, rrb2)
        q = slice((p % 4) * piece, (p % 4 + 1) * piece)
        main = (own[0, :, q].astype(F32) + left[:, q].astype(F32) + right[:, q].astype(F32)) * slot_weight
        value = jnp.concatenate([main, tail], axis=0)
        high = value.astype(BF16)
        low = (value - high.astype(F32)).astype(BF16)
        m = jnp.concatenate([main16, pick[p]], axis=0)
        spread = dot(m, high, TN_DIMS) + dot(m, low, TN_DIMS)
        out[:, at] = (gbuf[:, at].astype(F32) + spread).astype(BF16)

    for copy in copies:
        copy.wait_send()


def solution(mesh):
    def on_device(grad_out, parked_inputs, route_ids, route_probs, flight_expert, w_gate, w_up, w_down):
        features = grad_out.shape[1]
        half = features // 2
        hc = half // 2
        piece = half // PIECES
        vmem = pltpu.VMEM
        scratch = [
            vmem((TOK, half), BF16), vmem((TOK, half), BF16),
            vmem((ROWS, half), BF16), vmem((ROWS, half), BF16),
            vmem((256, piece), BF16), vmem((256, piece), BF16),
            vmem((3, FFD, half), BF16), vmem((3, 3, 2, FFD, half), BF16), vmem((3, FFD, half), BF16),
            vmem((ROWS, half), F32),
            vmem((5, ROWS, 384), F32), vmem((5, ROWS, 384), F32),
            vmem((ROWS, 256), BF16),
            vmem((4, 144, hc), BF16), vmem((4, 128, hc), BF16),
            vmem((64, hc), BF16), vmem((80, hc), BF16), vmem((144, hc), BF16), vmem((144, hc), BF16),
            vmem((64, hc), BF16), vmem((64, hc), BF16), vmem((128, hc), BF16), vmem((128, hc), BF16),
            vmem((4, 32, hc), BF16), vmem((4, 32, hc), BF16),
            vmem((16, hc), BF16), vmem((16, hc), BF16), vmem((32, hc), BF16), vmem((32, hc), BF16),
            vmem((16, hc), BF16), vmem((16, hc), BF16), vmem((32, hc), BF16), vmem((32, hc), BF16),
            vmem((4, 16, piece), BF16),
            vmem((16, piece), BF16), vmem((16, piece), BF16), vmem((16, piece), BF16),
            pltpu.SemaphoreType.DMA((NUM_SEMS,)), pltpu.SemaphoreType.DMA((NUM_SEMS,)),
            pltpu.SemaphoreType.DMA((5,)),
        ]
        any_space = pl.BlockSpec(memory_space=pl.ANY)
        in_vmem = pl.BlockSpec(memory_space=pltpu.VMEM)

        def body(*refs):
            kernel(half, *refs)

        return pl.pallas_call(
            body,
            out_shape=jax.ShapeDtypeStruct((TOK, half), BF16),
            in_specs=[pl.BlockSpec(memory_space=pltpu.SMEM), in_vmem, in_vmem,
                      any_space, any_space, any_space, any_space, any_space],
            out_specs=in_vmem,
            scratch_shapes=scratch,
            compiler_params=pltpu.CompilerParams(
                collective_id=0, has_side_effects=True, vmem_limit_bytes=60 * 1024 * 1024),
            cost_estimate=pl.CostEstimate(
                flops=10 * ROWS * 8 * FFD * half, bytes_accessed=10_000_000, transcendentals=ROWS * 512),
            name="routed_swiglu_backward",
        )(flight_expert, route_ids.T, route_probs.T, grad_out, parked_inputs, w_gate.T, w_up.T, w_down)

    in_specs = (
        P("ep", None),
        P("swap", "ep", None),
        P("ep", None),
        P("ep", None),
        P(),
        P(None, "ep"),
        P(None, "ep"),
        P("ep", None),
    )
    return jax.shard_map(
        on_device, mesh=mesh, in_specs=in_specs, out_specs=P("ep", "swap"), check_vma=False
    )
```

time: 465 us -> 139 us (0.30); the launches traced: 457 us -> 138 us
  waiting for transfers between devices: 277 us -> 0 us
  Pallas kernels: 0 us -> 136 us
  starting transfers between devices: 60.1 us -> 0 us
  matrix products: 46.4 us -> 0 us
  other arithmetic: 41.8 us -> 0 us
  local copies, waits for them, and re-layouts: 29.3 us -> 2.06 us
    ppermute x23 -> x0, waiting for transfers between devices: 277 us -> none  [partner_2(): return lax.ppermute(value, axis, pairs)]
    pallas_call x0 -> x1, Pallas kernels: none -> 136 us  [on_device(): pl.pallas_call(body, out_shape=jax.ShapeDtypeStruct((TOK, half), BF16), i...]
    ppermute x23 -> x0, starting transfers between devices: 60.1 us -> none  [partner_2(): return lax.ppermute(value, axis, pairs)]
    dot_general x5 -> x0, matrix products: 46.4 us -> none  [the longest x1 24.2 us: on_device(): lax.dot_general(d_gate, gate_cols, contract, preferred_element_type=jnp.f...]
    select_n x16 -> x0, other arithmetic: 27.4 us -> none  [the longest x15 24 us: join_by_bit(): return jnp.where(upper == 1, high_first, low_first)]
    select_n x9 -> x0, local copies, waits for them, and re-layouts: 16.6 us -> none  [the longest x8 14 us: join_by_bit(): return jnp.where(upper == 1, high_first, low_first)]
    add x4 -> x0, other arithmetic: 6.65 us -> none  [on_device(): keeping + partner_2(sending.astype(jnp.bfloat16), 'ep', bit).astype(sendi...]
    convert_element_type x5 -> x0, other arithmetic: 6.31 us -> none  [the longest x4 6.29 us: on_device(): sending.astype(jnp.bfloat16)]
  transfers between devices with their start and end apart: 23 -> 0, of which waited for: 14 -> 0; matrix products, arithmetic and copies ran while one was open for 14% -> 0% of each run, Pallas kernels for 0% -> 0%
where the time goes in v1:
time: 139 us; the launch traced here: 138 us
  Pallas kernels  136 us (98%)
  local copies, waits for them, and re-layouts  2.06 us (1%)
    pallas_call x1, Pallas kernels, on_device(): pl.pallas_call(body, out_shape=jax.ShapeDtypeStruct((TOK, half), BF16), i...  136 us

profile of v1, /device:TPU:1, one launch (start us, length us, event | category | flops | bytes accessed | tf_op | source)
XLA Modules:
  0.0 138.5 jit_solution(1154542009606149383)
XLA Ops:
  0.7 135.7 %routed_swiglu_backward.1 = bf16[128,3072]{1,0:T(8,128)(2,1)} custom-call(s32[1]{0:T(128)S(6)} %copy.10.refs_0_, s32[2,128]{1,0:T(2,128)} %bitcast.6, f32[2,128]{1,0:T(2,128)} %bitcast.7, bf16[128,6144]{1,0:T(8,128)(2,1)} %refs_3_.1, bf16[1,128,3072]{2,1,0:T(8,128)(2,1)} %refs_4_.1, bf16[64,6144]{1,0:T(8,128)(2,1)} %bitcast.4, bf16[64,6144]{1,0:T(8,128)(2,1)} %bitcast.5, ...), custom_call_target="tpu_custom_call" | custom-call | flops 8556380160 | bytes 10000000 | tf_op jit(solution)/shard_map/routed_swiglu_backward/pallas_call | solution.py:421
  136.4 2.1 %copy.11 = bf16[128,3072]{1,0:T(8,128)(2,1)} copy(bf16[128,3072]{1,0:T(8,128)(2,1)} %routed_swiglu_backward.1) | data formatting | bytes 1572864

commit v2 on v1

--- a/solution.py
+++ b/solution.py
@@ -17,7 +17,7 @@
 ROWS = 16 * CAP
 TAIL0 = 16 * MAIN
 PIECES = 8
-NUM_SEMS = 112
+NUM_SEMS = 128
 NT_DIMS = (((1,), (1,)), ((), ()))
 NN_DIMS = (((1,), (0,)), ((), ()))
 TN_DIMS = (((0,), (0,)), ((), ()))
@@ -33,9 +33,10 @@
 
 def kernel(half, fe, ids, probs, grad, parked, wg, wu, wd, out,
            gbuf, pbuf, rx, rdy, tx, tdy, w0, wp, wf, acc, ps, pr, dbuf,
-           sa, sb, rta, rba, rla, rra, rtb, rbb, rlb, rrb,
-           sa2, sb2, rta2, rba2, rla2, rra2, rtb2, rbb2, rlb2, rrb2,
-           t2, rtt, rlt, rrt, send_sem, recv_sem, local_sem):
+           sa_0, rta_0, rba_0, rla_0, rra_0, sa_1, rta_1, rba_1, rla_1, rra_1,
+           sb_0, rtb_0, rbb_0, rlb_0, rrb_0, sb_1, rtb_1, rbb_1, rlb_1, rrb_1,
+           sa2_0, ra2_0, sa2_1, ra2_1, sb2_0, rb2_0, sb2_1, rb2_1,
+           t1, t1r, t2, t2r, send_sem, recv_sem, local_sem):
     piece = half // PIECES
     hc = half // 2
     core = lax.axis_index("swap")
@@ -51,6 +52,10 @@
     xp, xm = chip(1, 0, 0), chip(-1, 0, 0)
     yp, ym = chip(0, 1, 0), chip(0, -1, 0)
     zp, zm = chip(0, 0, 1), chip(0, 0, -1)
+    xf, yf = chip(2, 0, 0), chip(0, 2, 0)
+    a_refs = [(sa_0, rta_0, rba_0, rla_0, rra_0), (sa_1, rta_1, rba_1, rla_1, rra_1)]
+    b_refs = [(sb_0, rtb_0, rbb_0, rlb_0, rrb_0), (sb_1, rtb_1, rbb_1, rlb_1, rrb_1)]
+    sa2, ra2, sb2, rb2 = (sa2_0, sa2_1), (ra2_0, ra2_1), (sb2_0, sb2_1), (rb2_0, rb2_1)
     other = (1 - core, ep)
 
     copies = []
@@ -73,9 +78,9 @@
         pltpu.make_async_copy(wd.at[:, cols], w0.at[2], local_sem.at[4]),
     ]
     barrier = pltpu.get_barrier_semaphore()
-    for peer in (xp, xm, yp, ym, zp, zm, other):
+    for peer in (xp, xm, yp, ym, zp, zm, xf, yf, other):
         pl.semaphore_signal(barrier, inc=1, device_id=peer, device_id_type=MESH)
-    for copy in local:
+    for copy in local[2:] + local[:2]:
         copy.start()
 
     hits = ids[...] == fe[0]
@@ -105,38 +110,38 @@
             t = t + dot(pick[p], src[:, p * piece:(p + 1) * piece])
         tails[0:16, :] = t.astype(BF16)
 
+    for copy in local[2:]:
+        copy.wait()
+    pl.semaphore_wait(barrier, 9)
+
+    gu, dn = pl.ds(0, 2), pl.ds(2, 1)
+
+    def ring(source, g, part, side):
+        return send(source, wp.at[g, part, side], zp if side == 0 else zm)
+
+    arrived = {}
+    for part, name in ((gu, "gu"), (dn, "dn")):
+        for side in (0, 1):
+            arrived[0, name, side] = ring(w0.at[part], 0, part, side)
+
+    def rows_of(s, n=1):
+        return pl.ds(MAIN * s, MAIN * n)
+
+    def tails_of(s, n=1):
+        return pl.ds(16 * s, 16 * n)
+
     local[0].wait()
     choose(pbuf, rx, tx)
-    local[1].wait()
-    choose(gbuf, rdy, tdy)
-    for copy in local[2:]:
-        copy.wait()
-    pl.semaphore_wait(barrier, 7)
-
-    def rows_of(s, n=1):
-        return pl.ds(MAIN * s, MAIN * n)
-
-    def tails_of(s, n=1):
-        return pl.ds(16 * s, 16 * n)
-
     px = [send(rx.at[rows_of(0)], rx.at[rows_of(3)], xp),
           send(rx.at[rows_of(0)], rx.at[rows_of(1)], xm),
           send(tx.at[tails_of(0)], tx.at[tails_of(3)], xp),
           send(tx.at[tails_of(0)], tx.at[tails_of(1)], xm)]
+    local[1].wait()
+    choose(gbuf, rdy, tdy)
     pd = [send(rdy.at[rows_of(0)], rdy.at[rows_of(12)], yp),
           send(rdy.at[rows_of(0)], rdy.at[rows_of(4)], ym),
           send(tdy.at[tails_of(0)], tdy.at[tails_of(12)], yp),
           send(tdy.at[tails_of(0)], tdy.at[tails_of(4)], ym)]
-
-    gu, dn = pl.ds(0, 2), pl.ds(2, 1)
-
-    def ring(source, g, part, side):
-        return send(source, wp.at[g, part, side], zp if side == 0 else zm)
-
-    arrived = {}
-    for part, name in ((gu, "gu"), (dn, "dn")):
-        for side in (0, 1):
-            arrived[0, name, side] = ring(w0.at[part], 0, part, side)
 
     def forward_rows(first, rows, tails, s3, s1, s2, plus, minus):
         for copy in first:
@@ -227,11 +232,12 @@
         used = pl.ds(0, 2 * width_of(g) + 128)
         return send(ps.at[g, :, used], pr.at[g, :, used], other)
 
-    def finish(g, copy):
-        copy.wait_recv()
+    def finish(g, begun, lo=0, hi=ROWS // 32):
+        for copy in begun:
+            copy.wait_recv()
         width = width_of(g)
 
-        @pl.loop(0, ROWS // 32)
+        @pl.loop(lo, hi)
         def _(m):
             rows = pl.ds(pl.multiple_of(m * 32, 32), 32)
             total = ps[g, rows, 0:2 * width + 128] + pr[g, rows, 0:2 * width + 128]
@@ -242,16 +248,16 @@
             d_gate = dhid * up * s * (1.0 + gate * (1.0 - s))
             dbuf[rows, 0:2 * width] = jnp.concatenate([d_gate, d_up], axis=1).astype(BF16)
 
-    tile = 512
-
-    def back_tiles(g, lo, hi):
+    tile = half // 6
+
+    def back_tiles(g):
         width = width_of(g)
 
-        @pl.loop(lo // tile, hi // tile)
+        @pl.loop(0, half // tile)
         def _(n):
             at = pl.ds(pl.multiple_of(n * tile, tile), tile)
-            if g == 0 or g == 4:
-                w = (w0 if g == 0 else wf)[0:2, :, at].reshape(2 * FFD, tile)
+            if g == 0:
+                w = w0[0:2, :, at].reshape(2 * FFD, tile)
             else:
                 w = wp[g - 1, 0:2, :, :, at].reshape(4 * FFD, tile)
             value = dot(dbuf[:, 0:2 * width], w)
@@ -260,18 +266,21 @@
             else:
                 acc[:, at] += value
 
-    def group(g):
+    def begin(g):
         partial_gate(g)
         partial_dhid(g)
-        copy = exchange(g)
-        finish(g, copy)
-        back_tiles(g, 0, half)
-
-    group(0)
-    group(1)
+        return exchange(g)
+
+    begun0, begun1 = begin(0), begin(1)
     forward_weights(2, "gu", gu)
+    finish(0, [begun0])
+    back_tiles(0)
+    finish(1, [begun1])
+    back_tiles(1)
     forward_weights(2, "dn", dn)
-    group(2)
+    begun2 = begin(2)
+    finish(2, [begun2])
+    back_tiles(2)
 
     def forward_far(name, part):
         result = []
@@ -285,70 +294,101 @@
     partial_gate(3)
     far_dn = forward_far("dn", dn)
     partial_dhid(3)
-    copy = exchange(3)
-    finish(3, copy)
-    back_tiles(3, 0, half)
+    finish(3, [exchange(3)])
+    back_tiles(3)
     for copy in far_gu:
         copy.wait_recv()
     partial_gate(4)
+    far_gate = send(ps.at[4, :, pl.ds(0, 128)], pr.at[4, :, pl.ds(0, 128)], other)
     for copy in far_dn:
         copy.wait_recv()
-    partial_dhid(4)
-    copy = exchange(4)
-    finish(4, copy)
+    far_dhid = []
+    for first, count in ((0, 288), (288, 256)):
+        dh = dot(rdy[first:first + count, :], wf[2], NT_DIMS)
+        ps[4, first:first + count, 128:256] = jnp.concatenate([dh, jnp.zeros_like(dh)], axis=1)
+        at = (4, pl.ds(first, count), pl.ds(128, 128))
+        far_dhid.append(send(ps.at[at], pr.at[at], other))
+    finish(4, [far_gate, far_dhid[0]], 0, 9)
+    finish(4, [far_dhid[1]], 9, 17)
 
     def add(a, b):
         return (a.astype(F32) + b.astype(F32)).astype(BF16)
 
-    def start_ring(unit, h, top, bottom, left, right, plus, minus):
-        size = unit.shape[1]
-        up, down = pl.ds(0, h), pl.ds(h, size - h)
-        return [send(unit.at[2, up], top, plus), send(unit.at[2, down], bottom, minus),
-                send(unit.at[1, down], left.at[down], plus), send(unit.at[3, up], right.at[up], minus)]
-
-    def turn_ring(begun, unit, h, top, bottom, left, right, plus, minus):
-        size = unit.shape[1]
-        up, down = pl.ds(0, h), pl.ds(h, size - h)
+    def start_ring(ring):
+        unit, top, bottom, left, right, plus, minus = ring
+        up, down = pl.ds(0, 64), pl.ds(64, 64)
+        return [send(unit.at[2, up], top, plus), send(unit.at[2, down], bottom, minus)]
+
+    def rest_ring(ring):
+        unit, top, bottom, left, right, plus, minus = ring
+        up, down = pl.ds(0, 64), pl.ds(64, 64)
+        return [send(unit.at[1, down], left.at[down], plus), send(unit.at[3, up], right.at[up], minus)]
+
+    def turn_ring(begun, ends, ring):
+        unit, top, bottom, left, right, plus, minus = ring
+        up, down = pl.ds(0, 64), pl.ds(64, 64)
         begun[0].wait_recv()
         unit[1, up] = add(unit[1, up], top[...])
-        ends = [begun[2], begun[3], send(unit.at[1, up], left.at[up], plus)]
+        ends.append(send(unit.at[1, up], left.at[up], plus))
         begun[1].wait_recv()
         unit[3, down] = add(unit[3, down], bottom[...])
         ends.append(send(unit.at[3, down], right.at[down], minus))
-        return ends
-
-    back_tiles(4, hc, half)
-    for j in (2, 1, 3, 0):
-        sb[j] = acc[128 * j:128 * j + 128, hc:half].astype(BF16)
-    ring_b = (sb, 64, rtb, rbb, rlb, rrb, yp, ym)
-    begun_b = start_ring(*ring_b)
-    back_tiles(4, 0, hc)
-    for i in (2, 1, 3, 0):
-        for j in range(4):
-            s = 4 * j + i
-            sa[i, 32 * j:32 * j + 32] = acc[MAIN * s:MAIN * s + MAIN, 0:hc].astype(BF16)
+
+    def second(ends, ring, unit, arrivals, plus, minus, far):
+        own, _, _, left, right, _, _ = ring
+        for copy in ends:
+            copy.wait_recv()
+        for k in (2, 1, 3, 0):
+            rows = slice(32 * k, 32 * k + 32)
+            unit[k] = (own[0, rows].astype(F32) + left[rows].astype(F32) + right[rows].astype(F32)).astype(BF16)
+        return scatter(unit, arrivals, plus, minus, far)
+
+    def scatter(unit, arrivals, plus, minus, far):
+        return [send(unit.at[2], arrivals.at[1], far),
+                send(unit.at[1], arrivals.at[0], plus), send(unit.at[3], arrivals.at[2], minus)]
+
+    rings_a = [a + (xp, xm) for a in a_refs]
+    rings_b = [b + (yp, ym) for b in b_refs]
+
+    def last_tiles(c, is_a):
+        n0, n1 = (0, 3) if c == 0 else (3, 4)
+        for n in range(n0, n1):
+            p = n if is_a else n + 4
+            at = slice(p * piece, (p + 1) * piece)
+            to = slice((n - n0) * piece, (n - n0 + 1) * piece)
+            value = acc[:, at] + dot(dbuf[:, 0:2 * FFD], wf[0:2, :, at].reshape(2 * FFD, piece))
+            for i in range(4):
+                for j in range(4):
+                    s = 4 * j + i
+                    block = value[MAIN * s:MAIN * s + MAIN].astype(BF16)
+                    if is_a:
+                        rings_a[c][0][i, 32 * j:32 * j + 32, to] = block
+                    else:
+                        rings_b[c][0][j, 32 * i:32 * i + 32, to] = block
+            acc[TAIL0:ROWS, at] = value[TAIL0:ROWS]
+
+    begun_a, begun_b, ends_a, ends_b = [], [], [], []
+    for c in range(2):
+        last_tiles(c, False)
+        begun_b.append(start_ring(rings_b[c]))
+        last_tiles(c, True)
+        begun_a.append(start_ring(rings_a[c]))
+    for i in range(4):
         t = acc[TAIL0 + 8 * i:TAIL0 + 8 * i + 8, :]
-        sa[i, 128:144] = jnp.concatenate([t[:, 0:hc], t[:, hc:half]], axis=0).astype(BF16)
-    ring_a = (sa, 64, rta, rba, rla, rra, xp, xm)
-    begun_a = start_ring(*ring_a)
-    ends_b = turn_ring(begun_b, *ring_b)
-    ends_a = turn_ring(begun_a, *ring_a)
-
-    for copy in ends_b:
-        copy.wait_recv()
-    for i in range(4):
-        rows = slice(32 * i, 32 * i + 32)
-        sb2[i] = (sb[0, rows].astype(F32) + rlb[rows].astype(F32) + rrb[rows].astype(F32)).astype(BF16)
-    ring_b2 = (sb2, 16, rtb2, rbb2, rlb2, rrb2, xp, xm)
-    begun_b2 = start_ring(*ring_b2)
-    for copy in ends_a:
-        copy.wait_recv()
-    for j in range(4):
-        rows = slice(32 * j, 32 * j + 32)
-        sa2[j] = (sa[0, rows].astype(F32) + rla[rows].astype(F32) + rra[rows].astype(F32)).astype(BF16)
-    ring_a2 = (sa2, 16, rta2, rba2, rla2, rra2, yp, ym)
-    begun_a2 = start_ring(*ring_a2)
-    tail = (sa[0, 128:144].astype(F32) + rla[128:144].astype(F32) + rra[128:144].astype(F32)).astype(BF16)
+        t1[i] = jnp.concatenate([t[:, 0:hc], t[:, hc:half]], axis=0).astype(BF16)
+    tail_ends = scatter(t1, t1r, xp, xm, xf)
+    for c in range(2):
+        ends_b.append(rest_ring(rings_b[c]))
+        ends_a.append(rest_ring(rings_a[c]))
+        turn_ring(begun_b[c], ends_b[c], rings_b[c])
+        turn_ring(begun_a[c], ends_a[c], rings_a[c])
+
+    for copy in tail_ends:
+        copy.wait_recv()
+    tail = t1[0].astype(F32)
+    for k in range(3):
+        tail = tail + t1r[k].astype(F32)
+    tail = tail.astype(BF16)
     row, col = iota((64, 16), 0), iota((64, 16), 1)
     p_of = (row % 16) // 2
     wanted = 8 * (p_of // 4) + 2 * (row // 16) + row % 2
@@ -357,30 +397,40 @@
         f = jnp.where((col == wanted) & (p_of % 4 == q), 1.0, 0.0).astype(BF16)
         packed = packed + dot(f, tail[:, q * piece:(q + 1) * piece])
     t2[...] = packed.astype(BF16).reshape(4, 16, piece)
-    tail_far = send(t2.at[2], rtt, yp)
-    tail_right = send(t2.at[3], rrt, ym)
-    ends_b2 = turn_ring(begun_b2, *ring_b2)
-    ends_a2 = turn_ring(begun_a2, *ring_a2)
-    tail_far.wait_recv()
-    t2[1] = add(t2[1], rtt[...])
-    tail_left = send(t2.at[1], rlt, yp)
+    tail_ends = scatter(t2, t2r, yp, ym, yf)
+
+    last_b, last_a = [], []
+    for c in range(2):
+        last_b.append(second(ends_b[c], rings_b[c], sb2[c], rb2[c], xp, xm, xf))
+        last_a.append(second(ends_a[c], rings_a[c], sa2[c], ra2[c], yp, ym, yf))
 
     slot_weight = 0.5 * jnp.sum(match_main * weight, axis=1, keepdims=True)
     tail_weight = 0.5 * jnp.sum(match_tail * weight, axis=1, keepdims=True)
-    for copy in ends_b2 + ends_a2 + [tail_right, tail_left]:
-        copy.wait_recv()
-    tail = (t2[0].astype(F32) + rlt[...].astype(F32) + rrt[...].astype(F32)) * tail_weight
-    for p in range(PIECES):
-        at = slice(p * piece, (p + 1) * piece)
-        own, left, right = (sa2, rla2, rra2) if p < 4 else (sb2, rlb2, rrb2)
-        q = slice((p % 4) * piece, (p % 4 + 1) * piece)
-        main = (own[0, :, q].astype(F32) + left[:, q].astype(F32) + right[:, q].astype(F32)) * slot_weight
-        value = jnp.concatenate([main, tail], axis=0)
-        high = value.astype(BF16)
-        low = (value - high.astype(F32)).astype(BF16)
-        m = jnp.concatenate([main16, pick[p]], axis=0)
-        spread = dot(m, high, TN_DIMS) + dot(m, low, TN_DIMS)
-        out[:, at] = (gbuf[:, at].astype(F32) + spread).astype(BF16)
+
+    def total(unit, arrivals, at=None):
+        if at is None:
+            return unit[0].astype(F32) + arrivals[0].astype(F32) + arrivals[1].astype(F32) + arrivals[2].astype(F32)
+        return (unit[0, :, at].astype(F32) + arrivals[0, :, at].astype(F32)
+                + arrivals[1, :, at].astype(F32) + arrivals[2, :, at].astype(F32))
+
+    for copy in tail_ends:
+        copy.wait_recv()
+    tail = total(t2, t2r) * tail_weight
+    for c in range(2):
+        for ends, unit, arrivals, p0 in ((last_b[c], sb2[c], rb2[c], 4), (last_a[c], sa2[c], ra2[c], 0)):
+            for copy in ends:
+                copy.wait_recv()
+            n0, n1 = (0, 3) if c == 0 else (3, 4)
+            for n in range(n0, n1):
+                p = p0 + n
+                at = slice(p * piece, (p + 1) * piece)
+                q = slice((n - n0) * piece, (n - n0 + 1) * piece)
+                value = jnp.concatenate([total(unit, arrivals, q) * slot_weight, tail], axis=0)
+                high = value.astype(BF16)
+                low = (value - high.astype(F32)).astype(BF16)
+                m = jnp.concatenate([main16, pick[p]], axis=0)
+                spread = dot(m, high, TN_DIMS) + dot(m, low, TN_DIMS)
+                out[:, at] = (gbuf[:, at].astype(F32) + spread).astype(BF16)
 
     for copy in copies:
         copy.wait_send()
@@ -390,9 +440,14 @@
     def on_device(grad_out, parked_inputs, route_ids, route_probs, flight_expert, w_gate, w_up, w_down):
         features = grad_out.shape[1]
         half = features // 2
-        hc = half // 2
-        piece = half // PIECES
+        hc, piece = half // 2, half // PIECES
         vmem = pltpu.VMEM
+        ring_scratch, second_scratch = [], []
+        for _ in range(2):
+            for width in (3 * piece, piece):
+                ring_scratch += [vmem((4, 128, width), BF16), vmem((64, width), BF16), vmem((64, width), BF16),
+                                 vmem((128, width), BF16), vmem((128, width), BF16)]
+                second_scratch += [vmem((4, 32, width), BF16), vmem((3, 32, width), BF16)]
         scratch = [
             vmem((TOK, half), BF16), vmem((TOK, half), BF16),
             vmem((ROWS, half), BF16), vmem((ROWS, half), BF16),
@@ -401,14 +456,9 @@
             vmem((ROWS, half), F32),
             vmem((5, ROWS, 384), F32), vmem((5, ROWS, 384), F32),
             vmem((ROWS, 256), BF16),
-            vmem((4, 144, hc), BF16), vmem((4, 128, hc), BF16),
-            vmem((64, hc), BF16), vmem((80, hc), BF16), vmem((144, hc), BF16), vmem((144, hc), BF16),
-            vmem((64, hc), BF16), vmem((64, hc), BF16), vmem((128, hc), BF16), vmem((128, hc), BF16),
-            vmem((4, 32, hc), BF16), vmem((4, 32, hc), BF16),
-            vmem((16, hc), BF16), vmem((16, hc), BF16), vmem((32, hc), BF16), vmem((32, hc), BF16),
-            vmem((16, hc), BF16), vmem((16, hc), BF16), vmem((32, hc), BF16), vmem((32, hc), BF16),
-            vmem((4, 16, piece), BF16),
-            vmem((16, piece), BF16), vmem((16, piece), BF16), vmem((16, piece), BF16),
+            *ring_scratch, *second_scratch,
+            vmem((4, 16, hc), BF16), vmem((3, 16, hc), BF16),
+            vmem((4, 16, piece), BF16), vmem((3, 16, piece), BF16),
             pltpu.SemaphoreType.DMA((NUM_SEMS,)), pltpu.SemaphoreType.DMA((NUM_SEMS,)),
             pltpu.SemaphoreType.DMA((5,)),
         ]

time: 139 us -> 134 us (0.964)
  Pallas kernels: 136 us -> 131 us
    pallas_call x1, Pallas kernels: 136 us -> 131 us  [on_device(): pl.pallas_call(body, out_shape=jax.ShapeDtypeStruct((TOK, half), BF16), i...]
where the time goes in v2:
time: 134 us
  Pallas kernels  131 us (98%)
  local copies, waits for them, and re-layouts  2.06 us (2%)
    pallas_call x1, Pallas kernels, on_device(): pl.pallas_call(body, out_shape=jax.ShapeDtypeStruct((TOK, half), BF16), i...  131 us

profile of v2, /device:TPU:1, one launch (start us, length us, event | category | flops | bytes accessed | tf_op | source)
XLA Modules:
  0.0 133.8 jit_solution(17875064872776105824)
XLA Ops:
  0.7 131.0 %routed_swiglu_backward.1 = bf16[128,3072]{1,0:T(8,128)(2,1)} custom-call(s32[1]{0:T(128)S(6)} %copy.10.refs_0_, s32[2,128]{1,0:T(2,128)} %bitcast.6, f32[2,128]{1,0:T(2,128)} %bitcast.7, bf16[128,6144]{1,0:T(8,128)(2,1)} %refs_3_.1, bf16[1,128,3072]{2,1,0:T(8,128)(2,1)} %refs_4_.1, bf16[64,6144]{1,0:T(8,128)(2,1)} %bitcast.4, bf16[64,6144]{1,0:T(8,128)(2,1)} %bitcast.5, ...), custom_call_target="tpu_custom_call" | custom-call | flops 8556380160 | bytes 10000000 | tf_op jit(solution)/shard_map/routed_swiglu_backward/pallas_call | solution.py:471
  131.7 2.1 %copy.11 = bf16[128,3072]{1,0:T(8,128)(2,1)} copy(bf16[128,3072]{1,0:T(8,128)(2,1)} %routed_swiglu_backward.1) | data formatting | bytes 1572864

commit v3 on v2

--- a/solution.py
+++ b/solution.py
@@ -36,7 +36,7 @@
            sa_0, rta_0, rba_0, rla_0, rra_0, sa_1, rta_1, rba_1, rla_1, rra_1,
            sb_0, rtb_0, rbb_0, rlb_0, rrb_0, sb_1, rtb_1, rbb_1, rlb_1, rrb_1,
            sa2_0, ra2_0, sa2_1, ra2_1, sb2_0, rb2_0, sb2_1, rb2_1,
-           t1, t1r, t2, t2r, send_sem, recv_sem, local_sem):
+           t1, t1top, t1bottom, t1left, t1right, t2, t2r, acc_dh, send_sem, recv_sem, local_sem):
     piece = half // PIECES
     hc = half // 2
     core = lax.axis_index("swap")
@@ -58,7 +58,11 @@
     sa2, ra2, sb2, rb2 = (sa2_0, sa2_1), (ra2_0, ra2_1), (sb2_0, sb2_1), (rb2_0, rb2_1)
     other = (1 - core, ep)
 
-    copies = []
+    copies, left_already = [], []
+
+    def gone(copy):
+        copy.wait_send()
+        left_already.append(copy)
 
     def send(src, dst, device):
         k = len(copies)
@@ -287,7 +291,12 @@
         for side in (0, 1):
             arrived[2, name, side].wait_recv()
             hid = pl.ds(32 * side, 32)
-            result.append(send(wp.at[2, part, side, hid], wf.at[part, hid], zp if side == 0 else zm))
+            to = zp if side == 0 else zm
+            if name == "gu":
+                result.append(send(wp.at[2, part, side, hid], wf.at[part, hid], to))
+            else:
+                result.append([send(wp.at[2, part, side, hid, pl.ds(lo, hc)], wf.at[part, hid, pl.ds(lo, hc)], to)
+                               for lo in (0, hc)])
         return result
 
     far_gu = forward_far("gu", gu)
@@ -300,11 +309,14 @@
         copy.wait_recv()
     partial_gate(4)
     far_gate = send(ps.at[4, :, pl.ds(0, 128)], pr.at[4, :, pl.ds(0, 128)], other)
-    for copy in far_dn:
-        copy.wait_recv()
+    for pair in far_dn:
+        pair[0].wait_recv()
+    acc_dh[...] = dot(rdy[:, 0:hc], wf[2, :, 0:hc], NT_DIMS)
+    for pair in far_dn:
+        pair[1].wait_recv()
     far_dhid = []
     for first, count in ((0, 288), (288, 256)):
-        dh = dot(rdy[first:first + count, :], wf[2], NT_DIMS)
+        dh = acc_dh[first:first + count, :] + dot(rdy[first:first + count, hc:half], wf[2, :, hc:half], NT_DIMS)
         ps[4, first:first + count, 128:256] = jnp.concatenate([dh, jnp.zeros_like(dh)], axis=1)
         at = (4, pl.ds(first, count), pl.ds(128, 128))
         far_dhid.append(send(ps.at[at], pr.at[at], other))
@@ -356,7 +368,7 @@
             p = n if is_a else n + 4
             at = slice(p * piece, (p + 1) * piece)
             to = slice((n - n0) * piece, (n - n0 + 1) * piece)
-            value = acc[:, at] + dot(dbuf[:, 0:2 * FFD], wf[0:2, :, at].reshape(2 * FFD, piece))
+            value = acc[0:TAIL0, at] + dot(dbuf[0:TAIL0, 0:2 * FFD], wf[0:2, :, at].reshape(2 * FFD, piece))
             for i in range(4):
                 for j in range(4):
                     s = 4 * j + i
@@ -365,30 +377,48 @@
                         rings_a[c][0][i, 32 * j:32 * j + 32, to] = block
                     else:
                         rings_b[c][0][j, 32 * i:32 * i + 32, to] = block
-            acc[TAIL0:ROWS, at] = value[TAIL0:ROWS]
 
     begun_a, begun_b, ends_a, ends_b = [], [], [], []
-    for c in range(2):
-        last_tiles(c, False)
-        begun_b.append(start_ring(rings_b[c]))
-        last_tiles(c, True)
-        begun_a.append(start_ring(rings_a[c]))
+    last_tiles(0, False)
+    begun_b.append(start_ring(rings_b[0]))
+    last_tiles(0, True)
+    begun_a.append(start_ring(rings_a[0]))
+
+    low_half, high_half = pl.ds(0, hc // 2), pl.ds(hc // 2, hc // 2)
+    tails = acc[TAIL0:ROWS, :] + dot(dbuf[TAIL0:ROWS, 0:2 * FFD], wf[0:2].reshape(2 * FFD, half))
     for i in range(4):
-        t = acc[TAIL0 + 8 * i:TAIL0 + 8 * i + 8, :]
+        t = tails[8 * i:8 * i + 8, :]
         t1[i] = jnp.concatenate([t[:, 0:hc], t[:, hc:half]], axis=0).astype(BF16)
-    tail_ends = scatter(t1, t1r, xp, xm, xf)
-    for c in range(2):
-        ends_b.append(rest_ring(rings_b[c]))
-        ends_a.append(rest_ring(rings_a[c]))
-        turn_ring(begun_b[c], ends_b[c], rings_b[c])
-        turn_ring(begun_a[c], ends_a[c], rings_a[c])
+    tail_top = send(t1.at[2, :, low_half], t1top, xp)
+    tail_bottom = send(t1.at[2, :, high_half], t1bottom, xm)
+
+    last_tiles(1, False)
+    begun_b.append(start_ring(rings_b[1]))
+    last_tiles(1, True)
+    begun_a.append(start_ring(rings_a[1]))
+
+    tail_ends = [send(t1.at[1, :, high_half], t1left.at[:, high_half], xp),
+                 send(t1.at[3, :, low_half], t1right.at[:, low_half], xm)]
+    for copy in begun_b[0] + begun_a[0]:
+        gone(copy)
+    ends_b.append(rest_ring(rings_b[0]))
+    ends_a.append(rest_ring(rings_a[0]))
+    tail_top.wait_recv()
+    t1[1, :, low_half] = add(t1[1, :, low_half], t1top[...])
+    tail_ends.append(send(t1.at[1, :, low_half], t1left.at[:, low_half], xp))
+    tail_bottom.wait_recv()
+    t1[3, :, high_half] = add(t1[3, :, high_half], t1bottom[...])
+    tail_ends.append(send(t1.at[3, :, high_half], t1right.at[:, high_half], xm))
+    turn_ring(begun_b[0], ends_b[0], rings_b[0])
+    turn_ring(begun_a[0], ends_a[0], rings_a[0])
+    ends_b.append(rest_ring(rings_b[1]))
+    ends_a.append(rest_ring(rings_a[1]))
+    turn_ring(begun_b[1], ends_b[1], rings_b[1])
+    turn_ring(begun_a[1], ends_a[1], rings_a[1])
 
     for copy in tail_ends:
         copy.wait_recv()
-    tail = t1[0].astype(F32)
-    for k in range(3):
-        tail = tail + t1r[k].astype(F32)
-    tail = tail.astype(BF16)
+    tail = (t1[0].astype(F32) + t1left[...].astype(F32) + t1right[...].astype(F32)).astype(BF16)
     row, col = iota((64, 16), 0), iota((64, 16), 1)
     p_of = (row % 16) // 2
     wanted = 8 * (p_of // 4) + 2 * (row // 16) + row % 2
@@ -433,7 +463,8 @@
                 out[:, at] = (gbuf[:, at].astype(F32) + spread).astype(BF16)
 
     for copy in copies:
-        copy.wait_send()
+        if not any(copy is other_copy for other_copy in left_already):
+            copy.wait_send()
 
 
 def solution(mesh):
@@ -457,8 +488,10 @@
             vmem((5, ROWS, 384), F32), vmem((5, ROWS, 384), F32),
             vmem((ROWS, 256), BF16),
             *ring_scratch, *second_scratch,
-            vmem((4, 16, hc), BF16), vmem((3, 16, hc), BF16),
+            vmem((4, 16, hc), BF16), vmem((16, hc // 2), BF16), vmem((16, hc // 2), BF16),
+            vmem((16, hc), BF16), vmem((16, hc), BF16),
             vmem((4, 16, piece), BF16), vmem((3, 16, piece), BF16),
+            vmem((ROWS, FFD), F32),
             pltpu.SemaphoreType.DMA((NUM_SEMS,)), pltpu.SemaphoreType.DMA((NUM_SEMS,)),
             pltpu.SemaphoreType.DMA((5,)),
         ]

time: 134 us -> 133 us (level)
  no operation moved by 1% of the time
where the time goes in v3:
time: 133 us
  Pallas kernels  130 us (98%)
  local copies, waits for them, and re-layouts  2.06 us (2%)
    pallas_call x1, Pallas kernels, on_device(): pl.pallas_call(body, out_shape=jax.ShapeDtypeStruct((TOK, half), BF16), i...  130 us

profile of v3, /device:TPU:1, one launch (start us, length us, event | category | flops | bytes accessed | tf_op | source)
XLA Modules:
  0.0 132.9 jit_solution(3226012438471501845)
XLA Ops:
  0.7 130.2 %routed_swiglu_backward.1 = bf16[128,3072]{1,0:T(8,128)(2,1)} custom-call(s32[1]{0:T(128)S(6)} %copy.10.refs_0_, s32[2,128]{1,0:T(2,128)} %bitcast.6, f32[2,128]{1,0:T(2,128)} %bitcast.7, bf16[128,6144]{1,0:T(8,128)(2,1)} %refs_3_.1, bf16[1,128,3072]{2,1,0:T(8,128)(2,1)} %refs_4_.1, bf16[64,6144]{1,0:T(8,128)(2,1)} %bitcast.4, bf16[64,6144]{1,0:T(8,128)(2,1)} %bitcast.5, ...), custom_call_target="tpu_custom_call" | custom-call | flops 8556380160 | bytes 10000000 | tf_op jit(solution)/shard_map/routed_swiglu_backward/pallas_call | solution.py:504
  130.8 2.1 %copy.11 = bf16[128,3072]{1,0:T(8,128)(2,1)} copy(bf16[128,3072]{1,0:T(8,128)(2,1)} %routed_swiglu_backward.1) | data formatting | bytes 1572864

commit v4 on v3

--- a/solution.py
+++ b/solution.py
@@ -177,6 +177,7 @@
             arrived[g, name, side] = ring(wp.at[g - 1, part, side], g, part, side)
 
     forward_weights(1, "gu", gu)
+    forward_weights(1, "dn", dn)
 
     for copy in px:
         copy.wait_recv()
@@ -191,7 +192,6 @@
         s, to = (4 * j + 3, xp) if j < 2 else (4 * j + 1, xm)
         last.append(send(rdy.at[rows_of(s)], rdy.at[rows_of(4 * j + 2)], to))
         last.append(send(tdy.at[tails_of(s)], tdy.at[tails_of(4 * j + 2)], to))
-    forward_weights(1, "dn", dn)
     for copy in last:
         copy.wait_recv()
 
@@ -275,13 +275,14 @@
         partial_dhid(g)
         return exchange(g)
 
-    begun0, begun1 = begin(0), begin(1)
+    begun0 = begin(0)
     forward_weights(2, "gu", gu)
+    begun1 = begin(1)
     finish(0, [begun0])
     back_tiles(0)
+    forward_weights(2, "dn", dn)
     finish(1, [begun1])
     back_tiles(1)
-    forward_weights(2, "dn", dn)
     begun2 = begin(2)
     finish(2, [begun2])
     back_tiles(2)
@@ -363,7 +364,7 @@
     rings_b = [b + (yp, ym) for b in b_refs]
 
     def last_tiles(c, is_a):
-        n0, n1 = (0, 3) if c == 0 else (3, 4)
+        n0, n1 = (0, 2) if c == 0 else (2, 4)
         for n in range(n0, n1):
             p = n if is_a else n + 4
             at = slice(p * piece, (p + 1) * piece)
@@ -450,7 +451,7 @@
         for ends, unit, arrivals, p0 in ((last_b[c], sb2[c], rb2[c], 4), (last_a[c], sa2[c], ra2[c], 0)):
             for copy in ends:
                 copy.wait_recv()
-            n0, n1 = (0, 3) if c == 0 else (3, 4)
+            n0, n1 = (0, 2) if c == 0 else (2, 4)
             for n in range(n0, n1):
                 p = p0 + n
                 at = slice(p * piece, (p + 1) * piece)
@@ -475,7 +476,7 @@
         vmem = pltpu.VMEM
         ring_scratch, second_scratch = [], []
         for _ in range(2):
-            for width in (3 * piece, piece):
+            for width in (2 * piece, 2 * piece):
                 ring_scratch += [vmem((4, 128, width), BF16), vmem((64, width), BF16), vmem((64, width), BF16),
                                  vmem((128, width), BF16), vmem((128, width), BF16)]
                 second_scratch += [vmem((4, 32, width), BF16), vmem((3, 32, width), BF16)]

time: 133 us -> 133 us (level)
  no operation moved by 1% of the time
where the time goes in v4:
time: 133 us
  Pallas kernels  130 us (98%)
  local copies, waits for them, and re-layouts  2.06 us (2%)
    pallas_call x1, Pallas kernels, on_device(): pl.pallas_call(body, out_shape=jax.ShapeDtypeStruct((TOK, half), BF16), i...  130 us

profile of v4, /device:TPU:1, one launch (start us, length us, event | category | flops | bytes accessed | tf_op | source)
XLA Modules:
  0.0 132.7 jit_solution(2912334882267268139)
XLA Ops:
  0.7 130.0 %routed_swiglu_backward.1 = bf16[128,3072]{1,0:T(8,128)(2,1)} custom-call(s32[1]{0:T(128)S(6)} %copy.10.refs_0_, s32[2,128]{1,0:T(2,128)} %bitcast.6, f32[2,128]{1,0:T(2,128)} %bitcast.7, bf16[128,6144]{1,0:T(8,128)(2,1)} %refs_3_.1, bf16[1,128,3072]{2,1,0:T(8,128)(2,1)} %refs_4_.1, bf16[64,6144]{1,0:T(8,128)(2,1)} %bitcast.4, bf16[64,6144]{1,0:T(8,128)(2,1)} %bitcast.5, ...), custom_call_target="tpu_custom_call" | custom-call | flops 8556380160 | bytes 10000000 | tf_op jit(solution)/shard_map/routed_swiglu_backward/pallas_call | solution.py:505
  130.6 2.1 %copy.11 = bf16[128,3072]{1,0:T(8,128)(2,1)} copy(bf16[128,3072]{1,0:T(8,128)(2,1)} %routed_swiglu_backward.1) | data formatting | bytes 1572864

commit v5 on v3

--- a/solution.py
+++ b/solution.py
@@ -286,6 +286,8 @@
     finish(2, [begun2])
     back_tiles(2)
 
+    before_far = len(copies)
+
     def forward_far(name, part):
         result = []
         for side in (0, 1):
@@ -309,6 +311,9 @@
         copy.wait_recv()
     partial_gate(4)
     far_gate = send(ps.at[4, :, pl.ds(0, 128)], pr.at[4, :, pl.ds(0, 128)], other)
+    for copy in copies[:before_far]:
+        gone(copy)
+    before_sums = len(copies)
     for pair in far_dn:
         pair[0].wait_recv()
     acc_dh[...] = dot(rdy[:, 0:hc], wf[2, :, 0:hc], NT_DIMS)
@@ -429,11 +434,15 @@
     t2[...] = packed.astype(BF16).reshape(4, 16, piece)
     tail_ends = scatter(t2, t2r, yp, ym, yf)
 
+    before_second = len(copies)
     last_b, last_a = [], []
     for c in range(2):
         last_b.append(second(ends_b[c], rings_b[c], sb2[c], rb2[c], xp, xm, xf))
         last_a.append(second(ends_a[c], rings_a[c], sa2[c], ra2[c], yp, ym, yf))
 
+    for copy in copies[before_sums:before_second]:
+        if not any(copy is other_copy for other_copy in left_already):
+            gone(copy)
     slot_weight = 0.5 * jnp.sum(match_main * weight, axis=1, keepdims=True)
     tail_weight = 0.5 * jnp.sum(match_tail * weight, axis=1, keepdims=True)
 

time: 133 us -> 133 us (level)
  no operation moved by 1% of the time
where the time goes in v5:
time: 133 us
  Pallas kernels  130 us (98%)
  local copies, waits for them, and re-layouts  2.06 us (2%)
    pallas_call x1, Pallas kernels, on_device(): pl.pallas_call(body, out_shape=jax.ShapeDtypeStruct((TOK, half), BF16), i...  130 us

profile of v5, /device:TPU:1, one launch (start us, length us, event | category | flops | bytes accessed | tf_op | source)
XLA Modules:
  0.0 132.7 jit_solution(8640670775344386725)
XLA Ops:
  0.7 130.0 %routed_swiglu_backward.1 = bf16[128,3072]{1,0:T(8,128)(2,1)} custom-call(s32[1]{0:T(128)S(6)} %copy.10.refs_0_, s32[2,128]{1,0:T(2,128)} %bitcast.6, f32[2,128]{1,0:T(2,128)} %bitcast.7, bf16[128,6144]{1,0:T(8,128)(2,1)} %refs_3_.1, bf16[1,128,3072]{2,1,0:T(8,128)(2,1)} %refs_4_.1, bf16[64,6144]{1,0:T(8,128)(2,1)} %bitcast.4, bf16[64,6144]{1,0:T(8,128)(2,1)} %bitcast.5, ...), custom_call_target="tpu_custom_call" | custom-call | flops 8556380160 | bytes 10000000 | tf_op jit(solution)/shard_map/routed_swiglu_backward/pallas_call | solution.py:513
  130.7 2.1 %copy.11 = bf16[128,3072]{1,0:T(8,128)(2,1)} copy(bf16[128,3072]{1,0:T(8,128)(2,1)} %routed_swiglu_backward.1) | data formatting | bytes 1572864

commit v6 on v5

--- a/solution.py
+++ b/solution.py
@@ -384,10 +384,10 @@
                         rings_b[c][0][j, 32 * i:32 * i + 32, to] = block
 
     begun_a, begun_b, ends_a, ends_b = [], [], [], []
+    last_tiles(0, True)
+    begun_a.append(start_ring(rings_a[0]))
     last_tiles(0, False)
     begun_b.append(start_ring(rings_b[0]))
-    last_tiles(0, True)
-    begun_a.append(start_ring(rings_a[0]))
 
     low_half, high_half = pl.ds(0, hc // 2), pl.ds(hc // 2, hc // 2)
     tails = acc[TAIL0:ROWS, :] + dot(dbuf[TAIL0:ROWS, 0:2 * FFD], wf[0:2].reshape(2 * FFD, half))
@@ -397,29 +397,29 @@
     tail_top = send(t1.at[2, :, low_half], t1top, xp)
     tail_bottom = send(t1.at[2, :, high_half], t1bottom, xm)
 
+    last_tiles(1, True)
+    begun_a.append(start_ring(rings_a[1]))
     last_tiles(1, False)
     begun_b.append(start_ring(rings_b[1]))
-    last_tiles(1, True)
-    begun_a.append(start_ring(rings_a[1]))
 
     tail_ends = [send(t1.at[1, :, high_half], t1left.at[:, high_half], xp),
                  send(t1.at[3, :, low_half], t1right.at[:, low_half], xm)]
     for copy in begun_b[0] + begun_a[0]:
         gone(copy)
+    ends_a.append(rest_ring(rings_a[0]))
     ends_b.append(rest_ring(rings_b[0]))
-    ends_a.append(rest_ring(rings_a[0]))
     tail_top.wait_recv()
     t1[1, :, low_half] = add(t1[1, :, low_half], t1top[...])
     tail_ends.append(send(t1.at[1, :, low_half], t1left.at[:, low_half], xp))
     tail_bottom.wait_recv()
     t1[3, :, high_half] = add(t1[3, :, high_half], t1bottom[...])
     tail_ends.append(send(t1.at[3, :, high_half], t1right.at[:, high_half], xm))
+    turn_ring(begun_a[0], ends_a[0], rings_a[0])
     turn_ring(begun_b[0], ends_b[0], rings_b[0])
-    turn_ring(begun_a[0], ends_a[0], rings_a[0])
+    ends_a.append(rest_ring(rings_a[1]))
     ends_b.append(rest_ring(rings_b[1]))
-    ends_a.append(rest_ring(rings_a[1]))
+    turn_ring(begun_a[1], ends_a[1], rings_a[1])
     turn_ring(begun_b[1], ends_b[1], rings_b[1])
-    turn_ring(begun_a[1], ends_a[1], rings_a[1])
 
     for copy in tail_ends:
         copy.wait_recv()

time: 133 us -> 132 us (level)
  no operation moved by 1% of the time
where the time goes in v6:
time: 132 us
  Pallas kernels  130 us (98%)
  local copies, waits for them, and re-layouts  2.06 us (2%)
    pallas_call x1, Pallas kernels, on_device(): pl.pallas_call(body, out_shape=jax.ShapeDtypeStruct((TOK, half), BF16), i...  130 us

profile of v6, /device:TPU:1, one launch (start us, length us, event | category | flops | bytes accessed | tf_op | source)
XLA Modules:
  0.0 132.2 jit_solution(10038211066037575660)
XLA Ops:
  0.7 129.5 %routed_swiglu_backward.1 = bf16[128,3072]{1,0:T(8,128)(2,1)} custom-call(s32[1]{0:T(128)S(6)} %copy.10.refs_0_, s32[2,128]{1,0:T(2,128)} %bitcast.6, f32[2,128]{1,0:T(2,128)} %bitcast.7, bf16[128,6144]{1,0:T(8,128)(2,1)} %refs_3_.1, bf16[1,128,3072]{2,1,0:T(8,128)(2,1)} %refs_4_.1, bf16[64,6144]{1,0:T(8,128)(2,1)} %bitcast.4, bf16[64,6144]{1,0:T(8,128)(2,1)} %bitcast.5, ...), custom_call_target="tpu_custom_call" | custom-call | flops 8556380160 | bytes 10000000 | tf_op jit(solution)/shard_map/routed_swiglu_backward/pallas_call | solution.py:513
  130.2 2.1 %copy.11 = bf16[128,3072]{1,0:T(8,128)(2,1)} copy(bf16[128,3072]{1,0:T(8,128)(2,1)} %routed_swiglu_backward.1) | data formatting | bytes 1572864
